TPU v7x, 128 devices: a whole 4x4x4 slice. The times are simulated.
128 devices in a mesh: dap: 8 (over z, y_lo), samp: 16 (over x, y_hi, core).
Axes of the slice: x: 4, y: 4 (y_hi: 2, y_lo: 2; y = y_hi * 2 + y_lo), z: 4, core: 2. Of those that a mesh axis runs over, the one named last changes fastest.
Arguments:
- pair_rep: bfloat16 [512, 512, 128], P('dap', 'samp'), may hold values from -6 to 6
- single: bfloat16 [512, 384], P('dap'), may hold values from -6 to 6
- residue_type: int32 [512], replicated, may hold values from 0 to 31
- chain_id: int32 [512], replicated, may hold values from 0 to 3, never falling along the last dimension, each value on 1 to 256 neighbouring positions
- residue_index: int32 [512], replicated, may hold values from 1 to 1024, as said below
- noisy_pos: float32 [64, 3, 512], P('samp', None, 'dap'), may hold values from -6 to 6
- type_table: bfloat16 [32, 384], replicated, may hold values from -6 to 6
- relpos_table: bfloat16 [66, 128], replicated, may hold values from -6 to 6
- tri_proj: bfloat16 [128, 512], replicated, may hold values from -0.5 to 0.5
- tri_gate: bfloat16 [128, 128], replicated, may hold values from -0.5 to 0.5
- tri_out: bfloat16 [128, 128], replicated, may hold values from -0.5 to 0.5
- bias_proj: bfloat16 [128, 16], replicated
- single_proj: bfloat16 [384, 768], replicated, may hold values from -0.3125 to 0.3125
- pos_proj: float32 [3, 768], replicated, may hold values from -3.5 to 3.5
- attn_proj: bfloat16 [768, 3072], replicated, may hold values from -0.21875 to 0.21875
- attn_out: bfloat16 [768, 768], replicated, may hold values from -0.21875 to 0.21875
- ff_in: bfloat16 [768, 3072], replicated, may hold values from -0.21875 to 0.21875
- ff_out: bfloat16 [1536, 768], replicated, may hold values from -0.15625 to 0.15625
- coord_out: bfloat16 [3, 768], replicated, may hold values from -0.21875 to 0.21875
Outputs:
- pair_next: bfloat16 [512, 512, 128], P('dap', 'samp')
- positions: float32 [64, 3, 512], P('samp', None, 'dap')
Inputs may be any that keep to these rules, and one draw needn't show every extreme that they name: `residue_index`: rises by 1 to 3 from each token to the next. `chain_id`: never falls along the tokens.
All inputs are finite; a program needn't handle non-finite values.
Results may differ from a plain program's by a relative error of at most 0.0094.
Values may be sent and summed in bfloat16 or wider, within the bound.
No kernel may reach another device: no remote copies, remote signals or barrier semaphores. Data moves between devices by JAX's collectives and lax.ppermute only.
A program may use at most 128 MiB of HBM per device.

v0:
```python
import jax
import jax.numpy as jnp
from jax import lax
from jax.sharding import PartitionSpec as P


def layer_norm(values):
    center = values - jnp.mean(values, axis=-1, keepdims=True)
    spread = jnp.mean(center * center, axis=-1, keepdims=True)
    return center * lax.rsqrt(spread + 1e-05)


def condition_rows(single_rows, type_rows, type_table, single_proj):
    type_ids = jnp.arange(type_table.shape[0], dtype=jnp.int32)
    type_hot = (type_rows[:, None] == type_ids[None, :]).astype(jnp.bfloat16)
    token_feat = single_rows.astype(jnp.float32) + jnp.dot(
        type_hot, type_table, preferred_element_type=jnp.float32
    )
    return jnp.dot(
        layer_norm(token_feat).astype(jnp.bfloat16), single_proj, preferred_element_type=jnp.float32
    )


def local(
    pair_rep,
    single,
    residue_type,
    chain_id,
    residue_index,
    noisy_pos,
    type_table,
    relpos_table,
    tri_proj,
    tri_gate,
    tri_out,
    bias_proj,
    single_proj,
    pos_proj,
    attn_proj,
    attn_out,
    ff_in,
    ff_out,
    coord_out,
):
    tok_rows, tok_cols, channels = pair_rep.shape
    tri_width = tri_out.shape[0]
    row_start = lax.axis_index("dap") * tok_rows
    col_start = lax.axis_index("samp") * tok_cols
    index_rows = lax.dynamic_slice_in_dim(residue_index, row_start, tok_rows)
    index_cols = lax.dynamic_slice_in_dim(residue_index, col_start, tok_cols)
    chain_rows = lax.dynamic_slice_in_dim(chain_id, row_start, tok_rows)
    chain_cols = lax.dynamic_slice_in_dim(chain_id, col_start, tok_cols)
    offset = jnp.clip(index_rows[:, None] - index_cols[None, :], -32, 32) + 32
    bins = jnp.where(chain_rows[:, None] == chain_cols[None, :], offset, 65)
    bin_ids = jnp.arange(relpos_table.shape[0], dtype=jnp.int32)
    one_hot = (bins[:, :, None] == bin_ids[None, None, :]).astype(jnp.bfloat16)
    embed = jnp.einsum("ijb,bc->ijc", one_hot, relpos_table, preferred_element_type=jnp.float32)
    pair_in = pair_rep.astype(jnp.float32) + embed
    pair_norm = layer_norm(pair_in).astype(jnp.bfloat16)
    projected = jnp.einsum("ijc,cd->ijd", pair_norm, tri_proj, preferred_element_type=jnp.float32)
    left = (
        jax.nn.sigmoid(projected[..., tri_width : 2 * tri_width]) * projected[..., :tri_width]
    ).astype(jnp.bfloat16)
    right = (
        jax.nn.sigmoid(projected[..., 3 * tri_width :])
        * projected[..., 2 * tri_width : 3 * tri_width]
    ).astype(jnp.bfloat16)
    right_all = lax.all_gather(right, "dap", axis=0, tiled=True)
    tri_sum = lax.psum_scatter(
        jnp.einsum("ikc,jkc->jic", left, right_all, preferred_element_type=jnp.float32),
        "samp",
        scatter_dimension=0,
        tiled=True,
    ).transpose(1, 0, 2)
    tri_norm = layer_norm(tri_sum).astype(jnp.bfloat16)
    update = jnp.einsum("ijc,cd->ijd", tri_norm, tri_out, preferred_element_type=jnp.float32)
    gating = jax.nn.sigmoid(
        jnp.einsum("ijc,cd->ijd", pair_norm, tri_gate, preferred_element_type=jnp.float32)
    )
    pair_next = (pair_in + gating * update).astype(jnp.bfloat16)
    full_rows = lax.all_gather(pair_next, "samp", axis=1, tiled=True)
    bias_norm = layer_norm(full_rows.astype(jnp.float32)).astype(jnp.bfloat16)
    pair_bias = jnp.einsum("ijc,ch->hij", bias_norm, bias_proj, preferred_element_type=jnp.float32)
    width = attn_out.shape[0]
    heads = bias_proj.shape[1]
    head_dim = width // heads
    ffn_width = ff_out.shape[0]
    samples_here = noisy_pos.shape[0]
    type_rows = lax.dynamic_slice_in_dim(residue_type, row_start, tok_rows)
    condition = condition_rows(single, type_rows, type_table, single_proj)
    act = condition[None] + jnp.einsum(
        "scn,ct->snt", noisy_pos, pos_proj, precision=lax.Precision.HIGHEST
    )
    normed = layer_norm(act).astype(jnp.bfloat16)
    mixed = jnp.einsum("snt,tu->snu", normed, attn_proj, preferred_element_type=jnp.float32)
    query_flat = mixed[..., :width].astype(jnp.bfloat16)
    key_part = mixed[..., width : 2 * width].astype(jnp.bfloat16)
    value_part = mixed[..., 2 * width : 3 * width].astype(jnp.bfloat16)
    gates = jax.nn.sigmoid(mixed[..., 3 * width :])
    key_all, value_all = (
        lax.all_gather(key_part, "dap", axis=1, tiled=True),
        lax.all_gather(value_part, "dap", axis=1, tiled=True),
    )
    query = query_flat.reshape(samples_here, tok_rows, heads, head_dim)
    total_keys = key_all.shape[1]
    key_all = key_all.reshape(samples_here, total_keys, heads, head_dim)
    value_all = value_all.reshape(samples_here, total_keys, heads, head_dim)
    scores = (
        jnp.einsum("sqhd,skhd->shqk", query, key_all, preferred_element_type=jnp.float32)
        * head_dim ** (-0.5)
        + pair_bias[None]
    )
    weights = jax.nn.softmax(scores, axis=-1).astype(jnp.bfloat16)
    attended = jnp.einsum(
        "shqk,skhd->sqhd", weights, value_all, preferred_element_type=jnp.float32
    ).reshape(samples_here, tok_rows, width)
    gated = (gates * attended).astype(jnp.bfloat16)
    act = act + jnp.einsum("snt,tu->snu", gated, attn_out, preferred_element_type=jnp.float32)
    hidden = jnp.einsum(
        "snt,tu->snu",
        layer_norm(act).astype(jnp.bfloat16),
        ff_in,
        preferred_element_type=jnp.float32,
    )
    inner = (jax.nn.silu(hidden[..., :ffn_width]) * hidden[..., ffn_width:]).astype(jnp.bfloat16)
    act = act + jnp.einsum("snf,ft->snt", inner, ff_out, preferred_element_type=jnp.float32)
    final = layer_norm(act).astype(jnp.bfloat16)
    shift = jnp.einsum("ct,snt->scn", coord_out, final, preferred_element_type=jnp.float32)
    return (pair_next, noisy_pos + shift)


def solution(mesh):
    in_specs = (
        P("dap", "samp", None),
        P("dap", None),
        P(),
        P(),
        P(),
        P("samp", None, "dap"),
        P(),
        P(),
        P(),
        P(),
        P(),
        P(),
        P(),
        P(),
        P(),
        P(),
        P(),
        P(),
        P(),
    )
    out_specs = (P("dap", "samp", None), P("samp", None, "dap"))
    return jax.shard_map(local, mesh=mesh, in_specs=in_specs, out_specs=out_specs, check_vma=False)
```

profile of v0, /device:TPU:1, one launch (start us, length us, event | category | flops | bytes accessed | tf_op | source)
XLA Modules:
  0.0 595.1 jit_solution(18379670358664518369)
XLA Ops:
  7.2 0.9 dynamic_slice.15
  8.1 0.8 dynamic_slice.17
  8.9 0.8 dynamic_slice.16
  9.7 0.8 dynamic_slice.18
  10.5 1.8 fusion.83
  12.5 0.6 multiply_reduce_fusion.1
  13.3 1.7 fusion.51
  15.0 1.5 fusion.34
  16.6 3.8 copy.92
  20.4 90.3 %all-gather.5.cloned.1.call-done = bf16[512,32,128]{2,1,0:T(8,128)(2,1)} async-done(((bf16[64,32,128]{2,1,0:T(8,128)(2,1)}), bf16[512,32,128]{2,1,0:T(8,128)(2,1)}) %all-gather.5.cloned.1.call-update) | async-done | bytes 4194320 | tf_op jit(solution)/shard_map/all_gather | solution.py:68
  110.6 8.6 %copy.91 = bf16[512,32,128]{0,1,2:T(8,128)(2,1)} copy(bf16[512,32,128]{2,1,0:T(8,128)(2,1)} %all-gather.5.cloned.1.call-done) | data formatting | bytes 8388608 | tf_op jit(solution)/shard_map/all_gather | solution.py:68
  119.2 10.6 %convolution_bitcast_fusion = f32[512,64,128]{0,1,2:T(8,128)} fusion(bf16[512,32,128]{0,1,2:T(8,128)(2,1)} %copy.91, bf16[64,32,128]{0,1,2:T(8,128)(2,1)} %copy.92), kind=kOutput, calls=%fused_computation.7 | convolution fusion | flops 268435456 | bytes 21495808 | tf_op jit(solution)/shard_map/ikc,jkc->jic/dot_general | solution.py:70
  129.8 16.8 %copy.93 = f32[512,64,128]{2,1,0:T(8,128)} copy(f32[512,64,128]{0,1,2:T(8,128)} %convolution_bitcast_fusion) | data formatting | bytes 33554432 | tf_op jit(solution)/shard_map/ikc,jkc->jic/transpose | solution.py:70
  146.7 0.8 dynamic_slice.19
  147.5 0.3 fusion.84
  148.0 1.3 fusion.68
  149.3 1.6 fusion.85
  151.0 0.2 multiply_reduce_fusion.4
  151.2 5.5 fusion.86
  156.7 1.0 fusion.82
  157.8 0.5 all-gather.7.cloned.1.call-update
  158.4 0.2 all-gather.11.cloned.1.call-start
  158.6 134.9 %reduce-scatter.2.cloned.1.call-done = f32[32,64,128]{2,1,0:T(8,128)} async-done(((f32[512,64,128]{2,1,0:T(8,128)}), f32[32,64,128]{2,1,0:T(8,128)}) %reduce-scatter.2.cloned.1.call-update) | async-done | bytes 1048592 | tf_op jit(solution)/shard_map/reduce_scatter | solution.py:69
  293.5 1.6 bitcast_reduce_fusion
  295.1 1.9 multiply_reduce_fusion
  297.0 1.8 multiply_convert_fusion
  298.8 0.4 fusion.52
  299.2 2.5 fusion.28
  301.7 2.2 copy.103
  303.9 61.2 %all-gather.9.cloned.1.call-done = bf16[4,512,768]{2,1,0:T(8,128)(2,1)} async-done(((bf16[4,64,768]{2,1,0:T(8,128)(2,1)}), bf16[4,512,768]{2,1,0:T(8,128)(2,1)}) %all-gather.9.cloned.1.call-update) | async-done | bytes 3145744 | tf_op jit(solution)/shard_map/all_gather | solution.py:101
  365.1 4.7 copy.97
  369.7 68.1 %all-gather.7.cloned.1.call-done = bf16[4,512,768]{2,1,0:T(8,128)(2,1)} async-done(((bf16[4,64,768]{2,1,0:T(8,128)(2,1)}), bf16[4,512,768]{2,1,0:T(8,128)(2,1)}) %all-gather.7.cloned.1.call-update) | async-done | bytes 3145744 | tf_op jit(solution)/shard_map/all_gather | solution.py:102
  437.8 4.7 copy.96
  442.5 78.4 %all-gather.11.cloned.1.call-done = bf16[64,512,128]{2,1,0:T(8,128)(2,1)} async-done(((bf16[64,32,128]{2,1,0:T(8,128)(2,1)}), bf16[64,512,128]{2,1,0:T(8,128)(2,1)}) %all-gather.11.cloned.1.call-update) | async-done | bytes 8388624 | tf_op jit(solution)/shard_map/all_gather | solution.py:81
  521.0 5.8 convert_reduce_fusion
  526.8 10.9 %fusion.3 = f32[64,512]{1,0:T(8,128)S(1)} fusion(bf16[64,512,128]{2,1,0:T(8,128)(2,1)} %all-gather.11.cloned.1.call-done, f32[64,512]{1,0:T(8,128)S(1)} %broadcast_multiply_fusion), kind=kLoop, calls=%fused_computation.5 | loop fusion | flops 16744448 | bytes 8650752 | tf_op jit(solution)/shard_map/reduce_sum | solution.py:9
  537.8 20.9 %fusion.19 = f32[16,64,512]{2,0,1:T(8,128)S(1)} fusion(bf16[64,512,128]{2,1,0:T(8,128)(2,1)S(1)} %bitcast.76, f32[64,512]{1,0:T(8,128)S(1)} %add_rsqrt_fusion, f32[64,512]{1,0:T(8,128)S(1)} %broadcast_multiply_fusion, bf16[128,16]{0,1:T(8,128)(2,1)S(1)} %copy-done.9), kind=kOutput, calls=%fused_computation.24 | convolution fusion | flops 150994944 | bytes 10752000 | tf_op jit(solution)/shard_map/ijc,ch->hij/dot_general | solution.py:83
  558.6 2.5 copy.99
  561.2 8.9 %fusion.87 = (f32[4,16,64]{2,1,0:T(8,128)S(1)}, f32[4,16,64,512]{3,2,1,0:T(8,128)}) fusion(f32[16,64,512]{2,1,0:T(8,128)} %copy.99, bf16[4,64,16,48]{1,3,2,0:T(8,128)(2,1)S(1)} %bitcast.78, bf16[4,512,16,48]{1,3,2,0:T(8,128)(2,1)} %bitcast.77), kind=kOutput, calls=%fused_computation.128 | convolution fusion | flops 209715712 | bytes 14041088 | tf_op jit(solution)/shard_map/sub | solution.py:113
  570.1 6.9 %fusion.16 = f32[4,16,48,64]{3,2,1,0:T(8,128)} fusion(bf16[4,512,16,48]{1,3,2,0:T(8,128)(2,1)} %bitcast.79, f32[4,16,64,512]{3,2,1,0:T(8,128)} %get-tuple-element.28, f32[4,16,64]{2,1,0:T(8,128)S(1)} %get-tuple-element.27), kind=kOutput, calls=%fused_computation.21 | convolution fusion | flops 205520896 | bytes 12337152 | tf_op jit(solution)/shard_map/shqk,skhd->sqhd/dot_general | solution.py:114
  577.0 2.8 copy.104
  579.8 2.4 fusion.88
  582.2 0.2 multiply_reduce_fusion.3
  582.5 3.8 fusion.10
  586.3 1.1 fusion.89
  587.4 0.2 multiply_reduce_fusion.2
  587.7 0.3 fusion.33
  588.0 0.6 copy.102
  (53 shorter events, 1.0 us)
Async XLA Ops:
  7.2 579.1 %copy-start = (bf16[1536,768]{1,0:T(8,128)(2,1)S(1)}, bf16[1536,768]{1,0:T(8,128)(2,1)}, u32[]{:S(2)}) copy-start(bf16[1536,768]{1,0:T(8,128)(2,1)} %param.36) | copy-start | bytes 7077892
  7.2 103.5 %all-gather.5.cloned.1.call-start = ((), (), s32[]{:S(2)}) async-start(), calls=%async_computation.1 | async-start | bytes 4718592 | tf_op jit(solution)/shard_map/all_gather | solution.py:68
  16.5 276.9 %reduce-scatter.2.cloned.1.call-start = ((), (), s32[]{:S(2)}) async-start(), calls=%async_computation.2 | async-start | bytes 17825792 | tf_op jit(solution)/shard_map/reduce_scatter | solution.py:69
  146.6 0.8 copy-start.4
  146.6 0.8 copy-start.7
  146.6 2.7 copy-start.5
  146.6 218.5 %all-gather.9.cloned.1.call-start = ((), (), s32[]{:S(2)}) async-start(), calls=%async_computation.4 | async-start | bytes 3538944 | tf_op jit(solution)/shard_map/all_gather | solution.py:101
  151.0 5.7 copy-start.1
  156.7 142.1 %copy-start.6 = (bf16[128,128]{1,0:T(8,128)(2,1)S(1)}, bf16[128,128]{1,0:T(8,128)(2,1)}, u32[]{:S(2)}) copy-start(bf16[128,128]{1,0:T(8,128)(2,1)} %param.29) | copy-start | bytes 98308
  157.8 280.0 %all-gather.7.cloned.1.call-start = ((), (), s32[]{:S(2)}) async-start(), calls=%async_computation.3 | async-start | bytes 3538944 | tf_op jit(solution)/shard_map/all_gather | solution.py:102
  158.4 362.6 %all-gather.11.cloned.1.call-start = ((), (), s32[]{:S(2)}) async-start(), calls=%async_computation.5 | async-start | bytes 8912896 | tf_op jit(solution)/shard_map/all_gather | solution.py:81
  521.0 16.8 %slice-start = ((s8[8388608]{0:T(1024)(128)(4,1)}), s8[4194304]{0:T(1024)(128)(4,1)S(1)}, s32[]{:S(2)}) async-start(s8[8388608]{0:T(1024)(128)(4,1)} %bitcast.75), calls=%async_computation.6 | async-start | bytes 8388608
  526.8 11.0 %slice-start.1 = ((s8[8388608]{0:T(1024)(128)(4,1)}), s8[4194304]{0:T(1024)(128)(4,1)S(1)}, s32[]{:S(2)}) async-start(s8[8388608]{0:T(1024)(128)(4,1)} %bitcast.75), calls=%async_computation.7 | async-start | bytes 8388608
  526.8 11.0 %copy-start.9 = (bf16[128,16]{0,1:T(8,128)(2,1)S(1)}, bf16[128,16]{0,1:T(8,128)(2,1)}, u32[]{:S(2)}) copy-start(bf16[128,16]{0,1:T(8,128)(2,1)} %param.30) | copy-start | bytes 12292
  558.6 2.6 copy-start.3
  570.1 9.7 %copy-start.2 = (f32[4,64,768]{2,1,0:T(8,128)S(1)}, f32[4,64,768]{2,1,0:T(8,128)}, u32[]{:S(2)}) copy-start(f32[4,64,768]{2,1,0:T(8,128)} %copy-done.1) | copy-start | bytes 2359300
  586.3 1.4 copy-start.8
Sparse Core Ops, SparseCore 0:
  16.7 93.9 all-gather.4
  146.8 146.6 reduce-scatter.1
  295.2 69.8 all-gather.8
  366.7 71.0 all-gather.6
  440.8 80.1 all-gather.10
where the time goes:
time: 597 us; the launch traced here: 595 us
  waiting for transfers between devices  433 us (73%)
  matrix products  70.1 us (12%)
  local copies, waits for them, and re-layouts  52 us (9%)
  other arithmetic  25.1 us (4%)
  between operations  14.1 us (2%)
    reduce_scatter x1, waiting for transfers between devices, local(): lax.psum_scatter(jnp.einsum('ikc,jkc->jic', left, right_all, preferred_el...  135 us
    all_gather x1, waiting for transfers between devices, local(): right_all = lax.all_gather(right, 'dap', axis=0, tiled=True)  90.3 us
    all_gather x1, waiting for transfers between devices, local(): full_rows = lax.all_gather(pair_next, 'samp', axis=1, tiled=True)  78.4 us
    all_gather x1, waiting for transfers between devices, local(): lax.all_gather(value_part, 'dap', axis=1, tiled=True)  68.1 us
    all_gather x1, waiting for transfers between devices, local(): lax.all_gather(key_part, 'dap', axis=1, tiled=True)  61.2 us
    dot_general x1, matrix products, local(): jnp.einsum('ijc,ch->hij', bias_norm, bias_proj, preferred_element_type=jn...  20.9 us
    transpose x1, local copies, waits for them, and re-layouts, local(): jnp.einsum('ikc,jkc->jic', left, right_all, preferred_element_type=jnp.fl...  16.8 us
    reduce_sum x7, other arithmetic, layer_norm(): spread = jnp.mean(center * center, axis=-1, keepdims=True)  14.2 us
  transfers between devices with their start and end apart: 5, of which 5 were waited for; matrix products, arithmetic and copies ran while one was open for 6% of the time, Pallas kernels for 0%

commit v1 on v0

v1 whole, which is shorter than its diff:
```python
import jax
import jax.numpy as jnp
from jax import lax
from jax.experimental import pallas as pl
from jax.experimental.pallas import tpu as pltpu
from jax.sharding import Mesh, PartitionSpec as P

F32 = jnp.float32
BF16 = jnp.bfloat16
AXES = ("dap", "sch", "core")
LOG2E = 1.4426950408889634
MIB = 1024 * 1024


def dot(a, b, dims):
    return lax.dot_general(a, b, ((dims[:1], dims[1:]), ((), ())), preferred_element_type=F32)


def sigmoid(x):
    return 0.5 * jnp.tanh(0.5 * x) + 0.5


def lane_iota(shape):
    return lax.broadcasted_iota(jnp.int32, shape, len(shape) - 1)


def swap_halves(a, b):
    low = lane_iota(a.shape) < 64
    return jnp.where(low, a, pltpu.roll(b, 64, 1)), jnp.where(low, pltpu.roll(a, 64, 1), b)


def call(kernel, out_shape, scratch=(), vmem=16, flops=0, nbytes=0, trans=0, **kw):
    return pl.pallas_call(
        kernel,
        out_shape=out_shape,
        scratch_shapes=list(scratch),
        compiler_params=pltpu.CompilerParams(vmem_limit_bytes=vmem * MIB),
        cost_estimate=pl.CostEstimate(flops=flops, bytes_accessed=nbytes, transcendentals=trans),
        **kw,
    )


VM = pl.BlockSpec(memory_space=pltpu.VMEM)
SM = pl.BlockSpec(memory_space=pltpu.SMEM)
ANY = pl.BlockSpec(memory_space=pl.ANY)


def pack_kernel(after_ref, single_ref, noisy_ref, out_ref, scr):
    core = lax.axis_index("core")
    rows = single_ref[pl.ds(pl.multiple_of(32 * core, 32), 32), :]
    scr[...] = jnp.zeros_like(scr)
    for c in range(3):
        scr[0, 4 * c : 4 * c + 4, 0:64] = noisy_ref[c]
    x = scr[0]
    high = x.astype(BF16).astype(F32)
    rest = x - high
    mid = rest.astype(BF16).astype(F32)
    low = rest - mid
    parts = [part.astype(BF16) for part in (high, mid, low)]
    for n in range(out_ref.shape[0]):
        out_ref[n, 0:32, :] = rows
        for k in range(3):
            out_ref[n, 32:48, 128 * k : 128 * (k + 1)] = parts[k]


def pair_rows(idx_s, chain_s, idx_v, chain_v, x_scr, table_ref):
    row_dev = lax.axis_index("dap")
    base = 32 * (2 * lax.axis_index("sch") + lax.axis_index("core"))
    lane = lane_iota((1, 128))
    odd = (row_dev % 2) == 1

    def rows_of(ref):
        row = ref[pl.ds(row_dev // 2, 1), :]
        turned = pltpu.roll(row, 64, 1)
        return jnp.where(lane < 64, jnp.where(odd, turned, row), jnp.where(odd, row, turned))

    idx_i, chain_i = rows_of(idx_v), rows_of(chain_v)
    bin_ids = lax.broadcasted_iota(jnp.int32, (table_ref.shape[0], 128), 0)

    def block(n):
        embed, rows = [], []
        for m in (2 * n, 2 * n + 1):
            idx_k = jnp.where(lane < 64, idx_s[base + m], idx_s[base + 16 + m])
            chain_k = jnp.where(lane < 64, chain_s[base + m], chain_s[base + 16 + m])
            bins = jnp.where(chain_i == chain_k, jnp.clip(idx_i - idx_k, -32, 32) + 32, 65)
            embed.append((bin_ids == bins).astype(F32).astype(BF16))
            rows += [x_scr[:, m, :], x_scr[:, 16 + m, :]]
        pin = jnp.concatenate(rows, axis=0) + dot(jnp.concatenate(embed, axis=1), table_ref[...], (0, 0))
        center = pin - jnp.mean(pin, axis=-1, keepdims=True)
        spread = jnp.mean(center * center, axis=-1, keepdims=True)
        return pin, (center * lax.rsqrt(spread + 1e-5)).astype(BF16)

    return block


def pair_kernel(idx_s, chain_s, idx_v, chain_v, pair_ref, table_ref, proj_ref, msg_ref, x_scr, msg_scr):
    x_scr[...] = pair_ref[...].astype(F32)
    proj_t = jnp.transpose(proj_ref[...].astype(F32)).astype(BF16)
    block = pair_rows(idx_s, chain_s, idx_v, chain_v, x_scr, table_ref)
    for n in range(8):
        _, norm = block(n)
        projected = dot(proj_t, norm, (1, 1))
        left = sigmoid(projected[128:256]) * projected[0:128]
        right = sigmoid(projected[384:512]) * projected[256:384]
        for half in range(2):
            cols = slice(128 * half, 128 * half + 128)
            msg_scr[:, 2 * n + half, :] = left[:, cols]
            msg_scr[:, 16 + 2 * n + half, :] = right[:, cols]
    msg_ref[...] = msg_scr[...].astype(BF16)


def gate_kernel(after_ref, idx_s, chain_s, idx_v, chain_v, pair_ref, table_ref, gate_w_ref, pin_ref, gate_ref, x_scr):
    x_scr[...] = pair_ref[...].astype(F32)
    block = pair_rows(idx_s, chain_s, idx_v, chain_v, x_scr, table_ref)
    for n in range(8):
        pin, norm = block(n)
        pin_ref[n] = pin
        gate_ref[n] = sigmoid(dot(norm, gate_w_ref[...], (1, 0)))


def tri_kernel(msg_ref, after_ref, after2_ref, out_ref, even_l, odd_l, even_r, odd_r):
    for pair in range(4):
        for which, (even, odd) in enumerate(((even_l, odd_l), (even_r, odd_r))):
            a = msg_ref[32 * pair : 32 * pair + 16, 16 * which : 16 * which + 16, :]
            b = msg_ref[32 * pair + 16 : 32 * pair + 32, 16 * which : 16 * which + 16, :]
            a = a.astype(F32).reshape(256, 128)
            b = b.astype(F32).reshape(256, 128)
            low, high = swap_halves(a, b)
            even[:, 128 * pair : 128 * pair + 128] = low.astype(BF16)
            odd[:, 128 * pair : 128 * pair + 128] = high.astype(BF16)
    for pair in range(4):
        cols = slice(128 * pair, 128 * pair + 128)
        total = dot(even_r[...], even_l[:, cols], (0, 0)) + dot(odd_r[...], odd_l[:, cols], (0, 0))
        total = total.reshape(16, 2, 16, 128)
        a = total[:, 0].reshape(256, 128)
        b = total[:, 1].reshape(256, 128)
        low, high = swap_halves(a, b)
        out_ref[32 * pair : 32 * pair + 16] = low.reshape(16, 16, 128).astype(BF16)
        out_ref[32 * pair + 16 : 32 * pair + 32] = high.reshape(16, 16, 128).astype(BF16)


def update_kernel(tri_ref, pin_ref, gate_ref, tri_out_ref, bias_w_ref, after_ref, next_ref, bias_ref, t_scr, x_scr, b_scr):
    t_scr[...] = tri_ref[...].astype(F32)
    for n in range(8):
        tri = jnp.concatenate([t_scr[:, 2 * n, :], t_scr[:, 2 * n + 1, :]], axis=1)
        center = tri - jnp.mean(tri, axis=0, keepdims=True)
        spread = jnp.mean(center * center, axis=0, keepdims=True)
        norm = (center * lax.rsqrt(spread + 1e-5)).astype(BF16)
        update = dot(norm, tri_out_ref[...], (0, 0))
        new = (pin_ref[n] + gate_ref[n] * update).astype(BF16).astype(F32)
        for half in range(2):
            x_scr[:, 2 * n + half, :] = new[128 * half : 128 * half + 64]
            x_scr[:, 16 + 2 * n + half, :] = new[128 * half + 64 : 128 * half + 128]
        center = new - jnp.mean(new, axis=-1, keepdims=True)
        spread = jnp.mean(center * center, axis=-1, keepdims=True)
        norm = (center * lax.rsqrt(spread + 1e-5)).astype(BF16)
        bias = dot(bias_w_ref[...], norm, (1, 1)) * LOG2E
        for half in range(2):
            b_scr[:, 2 * n + half, :] = bias[:, 128 * half : 128 * half + 128]
    next_ref[...] = x_scr[...].astype(BF16)
    for head in range(16):
        block = b_scr[head].astype(BF16)
        for group in range(8):
            bias_ref[head // 2, group, head % 2] = block


def front_kernel(after_ref, types_ref, recv_ref, type_table_ref, single_w_ref, pos_w_ref, attn_w_ref,
                 q_ref, k_ref, v_ref, g_ref, cond_scr, w_scr, coord_scr, pos_scr):
    step = pl.program_id(0)
    width = pos_w_ref.shape[1]

    @pl.when(step == 0)
    def _():
        head = 2 * lax.axis_index("dap") + lax.axis_index("core")
        pick_row = lax.broadcasted_iota(jnp.int32, (48, width), 0)
        pick = (lane_iota((48, width)) == pick_row + 48 * head).astype(F32).astype(BF16)
        for n in range(4):
            w_scr[48 * n : 48 * n + 48, :] = dot(pick, attn_w_ref[:, width * n : width * (n + 1)], (1, 1)).astype(BF16)
        hot = (lax.broadcasted_iota(jnp.int32, (32, 512), 0) == types_ref[...]).astype(F32).astype(BF16)
        types = dot(hot, type_table_ref[...], (0, 0))
        for d in range(16):
            feat = recv_ref[d, 0:32, :].astype(F32) + types[32 * d : 32 * d + 32]
            center = feat - jnp.mean(feat, axis=-1, keepdims=True)
            spread = jnp.mean(center * center, axis=-1, keepdims=True)
            norm = (center * lax.rsqrt(spread + 1e-5)).astype(BF16)
            cond = dot(norm, single_w_ref[...], (1, 0))
            cond_scr[32 * d : 32 * d + 32, :] = cond - jnp.mean(cond, axis=-1, keepdims=True)
        for core in range(2):
            for pair in range(4):
                for part in range(3):
                    cols = slice(128 * part, 128 * part + 128)
                    a = recv_ref[4 * pair + core, 32:48, cols].astype(F32)
                    b = recv_ref[4 * pair + 2 + core, 32:48, cols].astype(F32)
                    both = jnp.where(lane_iota((16, 128)) < 64, a, pltpu.roll(b, 64, 1)).astype(BF16)
                    for term, own in enumerate((0, 0, 1, 1, 0, 2)):
                        if own == part:
                            coord_scr[core, 16 * term : 16 * term + 16, 128 * pair : 128 * pair + 128] = both
        pos = pos_w_ref[...]
        pos = pos - jnp.mean(pos, axis=-1, keepdims=True)
        high = pos.astype(BF16).astype(F32)
        mid = (pos - high).astype(BF16).astype(F32)
        low = pos - high - mid
        low = low.astype(BF16).astype(F32)
        pos_scr[...] = jnp.zeros_like(pos_scr)
        for term, own in enumerate((0, 1, 0, 1, 2, 0)):
            for c in range(3):
                start = 16 * term + 4 * c
                pos_scr[start : start + 4, :] = jnp.broadcast_to((high, mid, low)[own][c : c + 1], (4, width))

    core, smp = step // 4, step % 4
    row = lax.broadcasted_iota(jnp.int32, (96, width), 0)
    chosen = jnp.where((row & 3) == smp, pos_scr[...], 0.0).astype(BF16)
    act = cond_scr[...] + dot(coord_scr[core], chosen, (0, 0))
    spread = jnp.mean(act * act, axis=-1, keepdims=True)
    norm = (act * lax.rsqrt(spread + 1e-5)).astype(BF16)
    mixed = dot(w_scr[...], norm, (1, 1))
    q_ref[0] = mixed[0:48].astype(BF16)
    k_ref[0] = jnp.transpose(mixed[48:96]).astype(BF16)
    v_ref[0] = mixed[96:144].astype(BF16)
    g_ref[0] = sigmoid(mixed[144:192])


def attn_kernel(bias_in_ref, q_ref, k_ref, v_ref, g_ref, out_ref, bias_scr):
    @pl.when(pl.program_id(0) == 0)
    def _():
        for pair in range(4):
            a = bias_in_ref[32 * pair : 32 * pair + 16].astype(F32).reshape(256, 128)
            b = bias_in_ref[32 * pair + 16 : 32 * pair + 32].astype(F32).reshape(256, 128)
            low, high = swap_halves(a, b)
            bias_scr[:, 0, :, 128 * pair : 128 * pair + 128] = low.reshape(16, 16, 128)
            bias_scr[:, 1, :, 128 * pair : 128 * pair + 128] = high.reshape(16, 16, 128)

    scale = 48.0 ** (-0.5) * LOG2E
    for half in range(2):
        cols = slice(256 * half, 256 * half + 256)
        bias = bias_scr[:, :, :, cols].reshape(512, 256)
        gated = []
        for n in range(2):
            scores = dot(k_ref[n], q_ref[n, :, cols], (1, 0)) * scale + bias
            top = jnp.max(scores, axis=0, keepdims=True)
            weights = jnp.exp2(scores - top)
            total = jnp.sum(weights, axis=0, keepdims=True)
            mixed = dot(v_ref[n], weights.astype(BF16), (1, 0))
            gated.append(g_ref[n, :, cols] * (mixed / total))
        for pair in range(2):
            low, high = swap_halves(*[g[:, 128 * pair : 128 * pair + 128] for g in gated])
            out_ref[4 * half + 2 * pair, 0] = low.astype(BF16)
            out_ref[4 * half + 2 * pair + 1, 0] = high.astype(BF16)


def tail_kernel(gated_ref, act0_ref, noisy_ref, attn_out_ref, ff_gate_ref, ff_up_ref, ff_out_ref, coord_ref,
                out_ref, act_scr, norm_scr):
    step = pl.program_id(0)

    @pl.when(step == 0)
    def _():
        act = act0_ref[...] + dot(gated_ref[...], attn_out_ref[...], (0, 0))
        act_scr[...] = act
        center = act - jnp.mean(act, axis=-1, keepdims=True)
        spread = jnp.mean(center * center, axis=-1, keepdims=True)
        norm_scr[...] = (center * lax.rsqrt(spread + 1e-5)).astype(BF16)

    norm = norm_scr[...]
    gate = dot(norm, ff_gate_ref[...], (1, 0))
    up = dot(norm, ff_up_ref[...], (1, 0))
    inner = (gate * sigmoid(gate) * up).astype(BF16)
    act_scr[...] += dot(inner, ff_out_ref[...], (1, 0))

    @pl.when(step == pl.num_programs(0) - 1)
    def _():
        act = act_scr[...]
        center = act - jnp.mean(act, axis=-1, keepdims=True)
        spread = jnp.mean(center * center, axis=-1, keepdims=True)
        final = (center * lax.rsqrt(spread + 1e-5)).astype(BF16)
        shift = dot(coord_ref[...], final, (1, 1))
        for c in range(3):
            moves = [shift[c : c + 1, 64 * n : 64 * n + 64] for n in range(4)]
            out_ref[c] = noisy_ref[c] + jnp.concatenate(moves, axis=0)


def layer_norm(values):
    center = values - jnp.mean(values, axis=-1, keepdims=True)
    spread = jnp.mean(center * center, axis=-1, keepdims=True)
    return center * lax.rsqrt(spread + 1e-05)


def condition_rows(single_rows, type_rows, type_table, single_proj):
    type_ids = jnp.arange(type_table.shape[0], dtype=jnp.int32)
    type_hot = (type_rows[:, None] == type_ids[None, :]).astype(BF16)
    token_feat = single_rows.astype(F32) + jnp.dot(type_hot, type_table, preferred_element_type=F32)
    return jnp.dot(layer_norm(token_feat).astype(BF16), single_proj, preferred_element_type=F32)


def local(
    pair_rep,
    single,
    residue_type,
    chain_id,
    residue_index,
    noisy_pos,
    type_table,
    relpos_table,
    tri_proj,
    tri_gate,
    tri_out,
    bias_proj,
    single_proj,
    pos_proj,
    attn_proj,
    attn_out,
    ff_in,
    ff_out,
    coord_out,
):
    sds = jax.ShapeDtypeStruct
    dap = lax.axis_index("dap")
    noisy = noisy_pos.transpose(1, 0, 2)

    rows_in = (residue_index, chain_id, residue_index.reshape(4, 128), chain_id.reshape(4, 128), pair_rep, relpos_table)
    rows_specs = [SM, SM, VM, VM, VM, VM]
    msg = call(
        pair_kernel, sds((128, 32, 128), BF16),
        [pltpu.VMEM((64, 32, 128), F32), pltpu.VMEM((128, 32, 128), F32)],
        flops=400_000_000, nbytes=1_700_000, trans=600_000,
        in_specs=rows_specs + [VM], out_specs=VM,
    )(*rows_in, tri_proj)
    by_channel = lax.all_to_all(msg, AXES, 0, 0, tiled=True)

    packed = call(
        pack_kernel, sds((16, 48, 384), BF16), [pltpu.VMEM((1, 16, 128), F32)], nbytes=700_000,
        in_specs=[ANY, VM, VM], out_specs=VM,
    )(msg, single, noisy)
    inputs_all = lax.all_to_all(packed, ("dap", "core"), 0, 0, tiled=True)
    pair_in, gates = call(
        gate_kernel, (sds((8, 256, 128), F32), sds((8, 256, 128), F32)), [pltpu.VMEM((64, 32, 128), F32)],
        flops=130_000_000, nbytes=3_000_000, trans=300_000,
        in_specs=[ANY] + rows_specs + [VM], out_specs=(VM, VM),
    )(msg, *rows_in, tri_gate)

    tri = call(
        tri_kernel, sds((128, 16, 128), BF16), [pltpu.VMEM((256, 512), BF16)] * 4,
        flops=270_000_000, nbytes=1_500_000, in_specs=[VM, ANY, ANY], out_specs=VM,
    )(by_channel, inputs_all, pair_in)
    tri_back = lax.all_to_all(tri, AXES, 0, 0, tiled=True)

    whole = lambda shape: pl.BlockSpec(shape, lambda i: (0,) * len(shape))
    per = lambda *shape: pl.BlockSpec((1,) + shape, lambda i: (i, 0, 0))
    query, key, value, head_gates = call(
        front_kernel,
        (sds((8, 48, 512), BF16), sds((8, 512, 48), BF16), sds((8, 48, 512), BF16), sds((8, 48, 512), F32)),
        [pltpu.VMEM((512, 768), F32), pltpu.VMEM((192, 768), BF16), pltpu.VMEM((2, 96, 512), BF16),
         pltpu.VMEM((96, 768), F32)],
        vmem=32, flops=2_500_000_000, nbytes=8_000_000, trans=300_000,
        grid=(8,),
        in_specs=[ANY, whole((1, 512)), whole((16, 48, 384)), whole((32, 384)), whole((384, 768)), whole((3, 768)),
                  whole((768, 3072))],
        out_specs=(per(48, 512), per(512, 48), per(48, 512), per(48, 512)),
    )(tri, residue_type.reshape(1, 512), inputs_all, type_table, single_proj, pos_proj, attn_proj)

    pair_next, bias = call(
        update_kernel,
        (sds((64, 32, 128), BF16), sds((8, 8, 2, 16, 128), BF16)),
        [pltpu.VMEM((128, 16, 128), F32), pltpu.VMEM((64, 32, 128), F32), pltpu.VMEM((16, 16, 128), F32)],
        flops=80_000_000, nbytes=4_000_000, in_specs=[VM] * 5 + [ANY], out_specs=(VM, VM),
    )(tri_back, pair_in, gates, tri_out, bias_proj.T, query)
    bias_all = lax.all_to_all(bias.reshape(128, 16, 128), AXES, 0, 0, tiled=True)

    two = lambda *shape: pl.BlockSpec((2,) + shape, lambda i: (i, 0, 0))
    gated = call(
        attn_kernel, sds((8, 2, 48, 256), BF16), [pltpu.VMEM((16, 2, 16, 512), F32)],
        flops=1_000_000_000, nbytes=2_500_000, trans=2_100_000,
        grid=(4,),
        in_specs=[whole((128, 16, 128)), two(48, 512), two(512, 48), two(48, 512), two(48, 512)],
        out_specs=pl.BlockSpec((8, 1, 48, 128), lambda i: (0, i // 2, 0, i % 2)),
    )(bias_all, query, key, value, head_gates)
    gated_rows = lax.all_to_all(gated.reshape(16, 48, 256), ("dap", "core"), 0, 0, tiled=True).reshape(768, 256)

    type_rows = lax.dynamic_slice_in_dim(residue_type, dap * 64, 64)
    condition = condition_rows(single, type_rows, type_table, single_proj)
    act0 = condition[None] + jnp.einsum("scn,ct->snt", noisy_pos, pos_proj, precision=lax.Precision.HIGHEST)
    chunk = 512
    positions = call(
        tail_kernel, sds((3, 4, 64), F32), [pltpu.VMEM((256, 768), F32), pltpu.VMEM((256, 768), BF16)],
        vmem=20, flops=2_100_000_000, nbytes=9_500_000, trans=400_000,
        grid=(1536 // chunk,),
        in_specs=[whole((768, 256)), whole((256, 768)), whole((3, 4, 64)), whole((768, 768)),
                  pl.BlockSpec((768, chunk), lambda i: (0, i)),
                  pl.BlockSpec((768, chunk), lambda i: (0, i + 1536 // chunk)),
                  pl.BlockSpec((chunk, 768), lambda i: (i, 0)),
                  whole((3, 768))],
        out_specs=whole((3, 4, 64)),
    )(gated_rows, act0.reshape(256, 768), noisy, attn_out, ff_in, ff_in, ff_out, coord_out)
    return (pair_next, positions.transpose(1, 0, 2))


def solution(mesh):
    fine = Mesh(mesh.devices.reshape(8, 8, 2), AXES)
    rep = P()
    samp = ("sch", "core")
    in_specs = (P("dap", samp, None), P("dap", None), rep, rep, rep, P(samp, None, "dap")) + (rep,) * 13
    out_specs = (P("dap", samp, None), P(samp, None, "dap"))
    return jax.shard_map(local, mesh=fine, in_specs=in_specs, out_specs=out_specs, check_vma=False)
```

time: 597 us -> 151 us (0.25)
  waiting for transfers between devices: 433 us -> 34 us
  matrix products: 70.1 us -> 3.17 us
  Pallas kernels: 0 us -> 38.4 us
  starting transfers between devices: 0.38 us -> 26.9 us
  local copies, waits for them, and re-layouts: 52 us -> 26.2 us
  other arithmetic: 25.1 us -> 1.08 us
  blocking collectives: 0 us -> 19 us
  between operations: 14.1 us -> 0.91 us
    all_gather x4 -> x0, waiting for transfers between devices: 298 us -> none  [the longest x1 90.3 us: local(): right_all = lax.all_gather(right, 'dap', axis=0, tiled=True)]
    reduce_scatter x1 -> x0, waiting for transfers between devices: 135 us -> none  [local(): lax.psum_scatter(jnp.einsum('ikc,jkc->jic', left, right_all, preferred_el...]
    dot_general x14 -> x2, matrix products: 59.5 us -> 2.32 us  [the longest x1 1.39 us: condition_rows(): jnp.dot(layer_norm(token_feat).astype(BF16), single_proj, preferred_eleme...]
    pallas_call x0 -> x8, Pallas kernels: none -> 38.4 us  [the longest x1 10.9 us: local(): call(front_kernel, (sds((8, 48, 512), BF16), sds((8, 512, 48), BF16), sds...]
    all_to_all x0 -> x4, waiting for transfers between devices: none -> 34 us  [the longest x1 15.3 us: local(): by_channel = lax.all_to_all(msg, AXES, 0, 0, tiled=True)]
    all_to_all x0 -> x4, starting transfers between devices: none -> 26.9 us  [the longest x1 9.9 us: local(): lax.all_to_all(bias.reshape(128, 16, 128), AXES, 0, 0, tiled=True)]
    unnamed x25 -> x78, local copies, waits for them, and re-layouts: 0.67 us -> 26.1 us
    all_to_all x0 -> x1, blocking collectives: none -> 19 us  [local(): inputs_all = lax.all_to_all(packed, ('dap', 'core'), 0, 0, tiled=True)]
  transfers between devices with their start and end apart: 5 -> 4, of which waited for: 5 -> 3; matrix products, arithmetic and copies ran while one was open for 6% -> 3% of each run, Pallas kernels for 0% -> 9%
where the time goes in v1:
time: 151 us; the launch traced here: 150 us
  Pallas kernels  38.4 us (25%)
  waiting for transfers between devices  34 us (23%)
  starting transfers between devices  26.9 us (18%)
  local copies, waits for them, and re-layouts  26.2 us (17%)
  blocking collectives  19 us (13%)
  matrix products  3.17 us (2%)
    unnamed x78, local copies, waits for them, and re-layouts  26.1 us
    all_to_all x1, blocking collectives, local(): inputs_all = lax.all_to_all(packed, ('dap', 'core'), 0, 0, tiled=True)  19 us
    all_to_all x1, waiting for transfers between devices, local(): by_channel = lax.all_to_all(msg, AXES, 0, 0, tiled=True)  15.3 us
    all_to_all x1, waiting for transfers between devices, local(): lax.all_to_all(bias.reshape(128, 16, 128), AXES, 0, 0, tiled=True)  12.4 us
    pallas_call x1, Pallas kernels, local(): call(front_kernel, (sds((8, 48, 512), BF16), sds((8, 512, 48), BF16), sds...  10.9 us
    all_to_all x1, starting transfers between devices, local(): lax.all_to_all(bias.reshape(128, 16, 128), AXES, 0, 0, tiled=True)  9.9 us
    pallas_call x1, Pallas kernels, local(): call(attn_kernel, sds((8, 2, 48, 256), BF16), [pltpu.VMEM((16, 2, 16, 512...  7.91 us
    all_to_all x1, starting transfers between devices, local(): by_channel = lax.all_to_all(msg, AXES, 0, 0, tiled=True)  7.28 us
  transfers between devices with their start and end apart: 4, of which 3 were waited for; matrix products, arithmetic and copies ran while one was open for 3% of the time, Pallas kernels for 9%

profile of v1, /device:TPU:1, one launch (start us, length us, event | category | flops | bytes accessed | tf_op | source)
XLA Modules:
  0.0 149.6 jit_solution(660264723118471135)
XLA Ops:
  0.7 1.0 copy-done.2
  1.7 0.9 copy-done.16
  2.6 0.7 copy-done.17
  3.3 0.7 copy-done.22
  4.0 0.7 copy-done.24
  4.7 5.6 %shard_map.194.after_ref = bf16[128,32,128]{2,1,0:T(8,128)(2,1)} custom-call(s32[512]{0:T(512)S(1)} %copy-done.22, s32[512]{0:T(512)S(1)} %copy-done.24, s32[4,128]{1,0:T(4,128)S(1)} %bitcast.19, s32[4,128]{1,0:T(4,128)S(1)} %bitcast.21, bf16[64,32,128]{2,1,0:T(8,128)(2,1)S(1)} %copy-done.2, bf16[66,128]{1,0:T(8,128)(2,1)S(1)} %copy-done.17, ...), custom_call_target="tpu_custom_call" | custom-call | flops 400000000 | bytes 1700000 | tf_op jit(solution)/shard_map/pallas_call | solution.py:321
  10.3 0.8 copy-done.14
  11.1 0.7 copy-done.19
  11.8 0.1 shard_map.195
  11.9 0.0 copy-start.27
  11.9 0.0 copy-start.28
  11.9 19.0 %all_to_all.25.after_ref.recv_ref = bf16[16,48,384]{2,1,0:T(8,128)(2,1)S(1)} all-to-all(bf16[16,48,384]{2,1,0:T(8,128)(2,1)S(1)} %shard_map.195), channel_id=1, replica_groups=mesh['dap'=8,'sch'=8,'core'=2] {'dap','core'}, dimensions={0} | all-to-all | bytes 1179648 | tf_op jit(solution)/shard_map/all_to_all | solution.py:333
  30.9 7.3 %all-to-all-start = ((bf16[128,32,128]{2,1,0:T(8,128)(2,1)}), bf16[128,32,128]{2,1,0:T(8,128)(2,1)S(1)}, u32[]{:S(2)}, u32[]{:S(2)}) async-start(bf16[128,32,128]{2,1,0:T(8,128)(2,1)} %shard_map.194.after_ref), calls=%async_computation | async-start | bytes 2097152 | tf_op jit(solution)/shard_map/all_to_all | solution.py:327
  38.3 2.6 %shard_map.196 = (f32[8,256,128]{2,1,0:T(8,128)S(1)}, f32[8,256,128]{2,1,0:T(8,128)S(1)}) custom-call(bf16[128,32,128]{2,1,0:T(8,128)(2,1)} %shard_map.194.after_ref, s32[512]{0:T(512)S(1)} %copy-done.23, s32[512]{0:T(512)S(1)} %copy-done.25, s32[4,128]{1,0:T(4,128)S(1)} %bitcast.20, s32[4,128]{1,0:T(4,128)S(1)} %bitcast.22, ...), custom_call_target="tpu_custom_call" | custom-call | flops 130000000 | bytes 3000000 | tf_op jit(solution)/shard_map/pallas_call | solution.py:334
  40.9 1.0 copy-done.7
  41.9 15.3 %all-to-all-done.msg_ref = bf16[128,32,128]{2,1,0:T(8,128)(2,1)S(1)} async-done(((bf16[128,32,128]{2,1,0:T(8,128)(2,1)}), bf16[128,32,128]{2,1,0:T(8,128)(2,1)S(1)}, u32[]{:S(2)}, u32[]{:S(2)}) %all-to-all-start) | async-done | bytes 1048608 | tf_op jit(solution)/shard_map/all_to_all | solution.py:327
  57.2 2.2 %shard_map.197.after_ref = bf16[128,16,128]{2,1,0:T(8,128)(2,1)} custom-call(bf16[128,32,128]{2,1,0:T(8,128)(2,1)S(1)} %all-to-all-done.msg_ref, bf16[16,48,384]{2,1,0:T(8,128)(2,1)S(1)} %all_to_all.25.after_ref.recv_ref, f32[8,256,128]{2,1,0:T(8,128)S(1)} %get-tuple-element.10.after2_ref.pin_ref), custom_call_target="tpu_custom_call" | custom-call | flops 270000000 | bytes 1500000 | tf_op jit(solution)/shard_map/pallas_call | solution.py:340
  59.3 4.6 %all-to-all-start.2 = ((bf16[128,16,128]{2,1,0:T(8,128)(2,1)}), bf16[128,16,128]{2,1,0:T(8,128)(2,1)S(1)}, u32[]{:S(2)}, u32[]{:S(2)}) async-start(bf16[128,16,128]{2,1,0:T(8,128)(2,1)} %shard_map.197.after_ref), calls=%async_computation.2 | async-start | bytes 1048576 | tf_op jit(solution)/shard_map/all_to_all | solution.py:344
  64.0 0.1 dynamic_slice.3
  64.1 0.9 fusion.6
  65.0 1.1 copy-done.9
  66.1 2.3 %copy-done.31 = bf16[768,3072]{1,0:T(8,128)(2,1)S(1)} copy-done((bf16[768,3072]{1,0:T(8,128)(2,1)S(1)}, bf16[768,3072]{1,0:T(8,128)(2,1)}, u32[]{:S(2)}) %copy-start.31) | copy-done | bytes 4718616
  68.4 10.9 %shard_map.198 = (bf16[8,48,512]{2,1,0:T(8,128)(2,1)S(1)}, bf16[8,512,48]{2,1,0:T(8,128)(2,1)S(1)}, bf16[8,48,512]{2,1,0:T(8,128)(2,1)S(1)}, f32[8,48,512]{2,1,0:T(8,128)S(1)}) custom-call(bf16[128,16,128]{2,1,0:T(8,128)(2,1)} %shard_map.197.after_ref, s32[1,512]{1,0:T(1,128)S(1)} %bitcast.24, bf16[16,48,384]{2,1,0:T(8,128)(2,1)S(1)} %all_to_all.25.after_ref.recv_ref, ...), custom_call_target="tpu_custom_call" | custom-call | flops 2500000000 | bytes 8000000 | tf_op jit(solution)/shard_map/pallas_call | solution.py:348
  79.3 0.7 copy-done.11
  80.0 1.0 copy-done.33
  81.0 0.9 copy-done.35
  81.9 0.7 copy-done.37
  82.6 0.8 copy-done.4
  83.4 1.0 copy-done.5
  84.5 1.2 copy-done.8
  85.7 1.0 copy-done.12
  86.7 3.3 %shard_map.199 = (bf16[64,32,128]{2,1,0:T(8,128)(2,1)}, bf16[8,8,2,16,128]{4,3,2,1,0:T(8,128)(2,1)S(1)}) custom-call(bf16[128,16,128]{2,1,0:T(8,128)(2,1)S(1)} %copy-done.5, f32[8,256,128]{2,1,0:T(8,128)S(1)} %get-tuple-element.10.after2_ref.pin_ref, f32[8,256,128]{2,1,0:T(8,128)S(1)} %copy-done.8, bf16[128,128]{1,0:T(8,128)(2,1)S(1)} %copy-done.21, ...), custom_call_target="tpu_custom_call" | custom-call | flops 80000000 | bytes 4000000 | tf_op jit(solution)/shard_map/pallas_call | solution.py:360
  90.0 0.8 copy-done.10
  90.8 9.9 %all-to-all-start.3 = ((bf16[128,16,128]{2,1,0:T(8,128)(2,1)}), bf16[128,16,128]{2,1,0:T(8,128)(2,1)S(1)}, u32[]{:S(2)}, u32[]{:S(2)}) async-start(bf16[128,16,128]{2,1,0:T(8,128)(2,1)} %bitcast.16), calls=%async_computation.3 | async-start | bytes 1048576 | tf_op jit(solution)/shard_map/all_to_all | solution.py:366
  100.7 1.1 multiply_reduce_fusion
  101.8 12.4 %all-to-all-done.3.bias_in_ref = bf16[128,16,128]{2,1,0:T(8,128)(2,1)S(1)} async-done(((bf16[128,16,128]{2,1,0:T(8,128)(2,1)}), bf16[128,16,128]{2,1,0:T(8,128)(2,1)S(1)}, u32[]{:S(2)}, u32[]{:S(2)}) %all-to-all-start.3) | async-done | bytes 524320 | tf_op jit(solution)/shard_map/all_to_all | solution.py:366
  114.2 1.0 copy-done.13
  115.2 1.2 copy-done.34
  116.5 1.1 copy-done.36
  117.6 1.0 copy-done.38
  118.6 7.9 %shard_map.200 = bf16[8,2,48,256]{3,2,1,0:T(8,128)(2,1)} custom-call(bf16[128,16,128]{2,1,0:T(8,128)(2,1)S(1)} %all-to-all-done.3.bias_in_ref, bf16[8,48,512]{2,1,0:T(8,128)(2,1)S(1)} %copy-done.13, bf16[8,512,48]{2,1,0:T(8,128)(2,1)S(1)} %copy-done.34, bf16[8,48,512]{2,1,0:T(8,128)(2,1)S(1)} %copy-done.38, f32[8,48,512]{2,1,0:T(8,128)S(1)} %copy-done.36), custom_call_target="tpu_custom_call" | custom-call | flops 1000000000 | bytes 2500000 | tf_op jit(solution)/shard_map/pallas_call | solution.py:369
  126.5 5.1 %all-to-all-start.4 = ((bf16[16,48,256]{2,1,0:T(8,128)(2,1)}), bf16[16,48,256]{2,1,0:T(8,128)(2,1)}, u32[]{:S(2)}, u32[]{:S(2)}) async-start(bf16[16,48,256]{2,1,0:T(8,128)(2,1)} %bitcast.6), calls=%async_computation.4 | async-start | bytes 786432 | tf_op jit(solution)/shard_map/all_to_all | solution.py:376
  131.6 1.4 fusion
  133.0 0.8 convolution_add_fusion
  133.8 6.3 %all-to-all-done.4 = bf16[16,48,256]{2,1,0:T(8,128)(2,1)} async-done(((bf16[16,48,256]{2,1,0:T(8,128)(2,1)}), bf16[16,48,256]{2,1,0:T(8,128)(2,1)}, u32[]{:S(2)}, u32[]{:S(2)}) %all-to-all-start.4) | async-done | bytes 393248 | tf_op jit(solution)/shard_map/all_to_all | solution.py:376
  140.2 2.3 %copy-done = bf16[768,3072]{1,0:T(8,128)(2,1)S(1)} copy-done((bf16[768,3072]{1,0:T(8,128)(2,1)S(1)}, bf16[768,3072]{1,0:T(8,128)(2,1)}, u32[]{:S(2)}) %copy-start) | copy-done | bytes 4718616
  142.5 1.3 copy-done.6
  143.8 5.8 %shard_map.201 = f32[3,4,64]{2,1,0:T(4,128)} custom-call(bf16[768,256]{1,0:T(8,128)(2,1)} %bitcast.7.gated_ref, f32[256,768]{1,0:T(8,128)S(1)} %bitcast.15, f32[3,4,64]{2,1,0:T(4,128)S(1)} %bitcast.18, bf16[768,768]{1,0:T(8,128)(2,1)S(1)} %copy-done.6, bf16[768,3072]{1,0:T(8,128)(2,1)S(1)} %copy-done, bf16[768,3072]{1,0:T(8,128)(2,1)S(1)} %copy-done, ...), custom_call_target="tpu_custom_call" | custom-call | flops 2100000000 | bytes 9500000 | tf_op jit(solution)/shard_map/pallas_call | solution.py:382
  (54 shorter events, 0.1 us)
Async XLA Ops:
  0.6 37.6 %copy-start.23 = (s32[512]{0:T(512)S(1)}, s32[512]{0:T(512)}, u32[]{:S(2)}) copy-start(s32[512]{0:T(512)} %idx_s.3) | copy-start | bytes 6148
  0.6 1.0 copy-start.2
  1.7 0.9 copy-start.16
  2.6 0.7 copy-start.17
  3.3 0.7 copy-start.22
  4.0 0.7 copy-start.24
  4.7 33.6 %copy-start.3 = (bf16[64,32,128]{2,1,0:T(8,128)(2,1)S(1)}, bf16[64,32,128]{2,1,0:T(8,128)(2,1)}, u32[]{:S(2)}) copy-start(bf16[64,32,128]{2,1,0:T(8,128)(2,1)} %pair_ref.3) | copy-start | bytes 1572868
  4.7 33.6 %copy-start.18 = (bf16[66,128]{1,0:T(8,128)(2,1)S(1)}, bf16[66,128]{1,0:T(8,128)(2,1)}, u32[]{:S(2)}) copy-start(bf16[66,128]{1,0:T(8,128)(2,1)} %table_ref.3) | copy-start | bytes 50692
  4.7 33.6 %copy-start.25 = (s32[512]{0:T(512)S(1)}, s32[512]{0:T(512)}, u32[]{:S(2)}) copy-start(s32[512]{0:T(512)} %chain_s.3) | copy-start | bytes 6148
  4.7 33.6 %copy-start.26 = (bf16[128,128]{1,0:T(8,128)(2,1)S(1)}, bf16[128,128]{1,0:T(8,128)(2,1)}, u32[]{:S(2)}) copy-start(bf16[128,128]{1,0:T(8,128)(2,1)} %gate_w_ref.1) | copy-start | bytes 98308
  10.3 0.8 copy-start.14
  11.1 0.7 copy-start.19
  11.9 52.1 %copy-start.32 = (s32[512]{0:T(512)S(1)}, s32[512]{0:T(512)}, u32[]{:S(2)}) copy-start(s32[512]{0:T(512)} %param.21) | copy-start | bytes 6148
  11.9 52.2 %copy-start.15 = (bf16[64,384]{1,0:T(8,128)(2,1)S(1)}, bf16[64,384]{1,0:T(8,128)(2,1)}, u32[]{:S(2)}) copy-start(bf16[64,384]{1,0:T(8,128)(2,1)} %single_ref.1) | copy-start | bytes 147460
  11.9 52.2 %copy-start.27 = (bf16[32,384]{1,0:T(8,128)(2,1)S(1)}, bf16[32,384]{1,0:T(8,128)(2,1)}, u32[]{:S(2)}) copy-start(bf16[32,384]{1,0:T(8,128)(2,1)} %type_table_ref.1) | copy-start | bytes 73732
  11.9 53.1 %copy-start.28 = (f32[3,768]{1,0:T(4,128)S(1)}, f32[3,768]{1,0:T(4,128)}, u32[]{:S(2)}) copy-start(f32[3,768]{1,0:T(4,128)} %pos_w_ref.1) | copy-start | bytes 27652
  30.9 26.2 %all-to-all-start = ((bf16[128,32,128]{2,1,0:T(8,128)(2,1)}), bf16[128,32,128]{2,1,0:T(8,128)(2,1)S(1)}, u32[]{:S(2)}, u32[]{:S(2)}) async-start(bf16[128,32,128]{2,1,0:T(8,128)(2,1)} %shard_map.194.after_ref), calls=%async_computation | async-start | bytes 2097152 | tf_op jit(solution)/shard_map/all_to_all | solution.py:327
  40.9 1.0 copy-start.7
  59.3 23.3 %all-to-all-start.2 = ((bf16[128,16,128]{2,1,0:T(8,128)(2,1)}), bf16[128,16,128]{2,1,0:T(8,128)(2,1)S(1)}, u32[]{:S(2)}, u32[]{:S(2)}) async-start(bf16[128,16,128]{2,1,0:T(8,128)(2,1)} %shard_map.197.after_ref), calls=%async_computation.2 | async-start | bytes 1048576 | tf_op jit(solution)/shard_map/all_to_all | solution.py:344
  63.9 19.5 %copy-start.21 = (bf16[128,128]{1,0:T(8,128)(2,1)S(1)}, bf16[128,128]{1,0:T(8,128)(2,1)}, u32[]{:S(2)}) copy-start(bf16[128,128]{1,0:T(8,128)(2,1)} %tri_out_ref.1) | copy-start | bytes 98308
  63.9 19.5 %copy-start.30 = (bf16[128,16]{0,1:T(8,128)(2,1)S(1)}, bf16[128,16]{0,1:T(8,128)(2,1)}, u32[]{:S(2)}) copy-start(bf16[128,16]{0,1:T(8,128)(2,1)} %param.30) | copy-start | bytes 12292
  65.0 1.1 copy-start.9
  66.1 2.3 %copy-start.31 = (bf16[768,3072]{1,0:T(8,128)(2,1)S(1)}, bf16[768,3072]{1,0:T(8,128)(2,1)}, u32[]{:S(2)}) copy-start(bf16[768,3072]{1,0:T(8,128)(2,1)} %attn_w_ref.1) | copy-start | bytes 14155780
  79.3 0.7 copy-start.11
  80.0 1.0 copy-start.33
  81.0 0.9 copy-start.35
  81.9 0.7 copy-start.37
  82.6 0.8 copy-start.4
  83.4 1.0 copy-start.5
  84.5 1.2 copy-start.8
  85.7 1.0 copy-start.12
  86.7 46.3 %copy-start.20 = (f32[4,3,64]{2,0,1:T(4,128)S(1)}, f32[4,3,64]{2,0,1:T(4,128)}, u32[]{:S(2)}) copy-start(f32[4,3,64]{2,0,1:T(4,128)} %param.24) | copy-start | bytes 9220
  86.7 53.5 %copy-start.1 = (bf16[1536,768]{1,0:T(8,128)(2,1)S(1)}, bf16[1536,768]{1,0:T(8,128)(2,1)}, u32[]{:S(2)}) copy-start(bf16[1536,768]{1,0:T(8,128)(2,1)} %ff_out_ref.1) | copy-start | bytes 7077892
  86.7 53.5 %copy-start.29 = (bf16[3,768]{1,0:T(4,128)(2,1)S(1)}, bf16[3,768]{1,0:T(4,128)(2,1)}, u32[]{:S(2)}) copy-start(bf16[3,768]{1,0:T(4,128)(2,1)} %coord_ref.1) | copy-start | bytes 13828
  90.0 0.8 copy-start.10
  90.8 23.4 %all-to-all-start.3 = ((bf16[128,16,128]{2,1,0:T(8,128)(2,1)}), bf16[128,16,128]{2,1,0:T(8,128)(2,1)S(1)}, u32[]{:S(2)}, u32[]{:S(2)}) async-start(bf16[128,16,128]{2,1,0:T(8,128)(2,1)} %bitcast.16), calls=%async_computation.3 | async-start | bytes 1048576 | tf_op jit(solution)/shard_map/all_to_all | solution.py:366
  114.2 1.0 copy-start.13
  115.2 1.2 copy-start.34
  116.4 1.1 copy-start.36
  117.6 1.0 copy-start.38
  126.5 13.7 %all-to-all-start.4 = ((bf16[16,48,256]{2,1,0:T(8,128)(2,1)}), bf16[16,48,256]{2,1,0:T(8,128)(2,1)}, u32[]{:S(2)}, u32[]{:S(2)}) async-start(bf16[16,48,256]{2,1,0:T(8,128)(2,1)} %bitcast.6), calls=%async_computation.4 | async-start | bytes 786432 | tf_op jit(solution)/shard_map/all_to_all | solution.py:376
  140.2 2.3 %copy-start = (bf16[768,3072]{1,0:T(8,128)(2,1)S(1)}, bf16[768,3072]{1,0:T(8,128)(2,1)}, u32[]{:S(2)}) copy-start(bf16[768,3072]{1,0:T(8,128)(2,1)} %ff_up_ref.1) | copy-start | bytes 14155780
  142.5 1.3 copy-start.6

commit v2 on v1

v2 whole, which is shorter than its diff:
```python
import jax
import jax.numpy as jnp
from jax import lax
from jax.experimental import pallas as pl
from jax.experimental.pallas import tpu as pltpu
from jax.sharding import Mesh, PartitionSpec as P

F32 = jnp.float32
BF16 = jnp.bfloat16
AXES = ("dap", "sch", "core")
LOG2E = 1.4426950408889634
MIB = 1024 * 1024


def dot(a, b, dims):
    return lax.dot_general(a, b, ((dims[:1], dims[1:]), ((), ())), preferred_element_type=F32)


def sigmoid(x):
    return 0.5 * jnp.tanh(0.5 * x) + 0.5


def lane_iota(shape):
    return lax.broadcasted_iota(jnp.int32, shape, len(shape) - 1)


def swap_halves(a, b):
    low = lane_iota(a.shape) < 64
    return jnp.where(low, a, pltpu.roll(b, 64, 1)), jnp.where(low, pltpu.roll(a, 64, 1), b)


def call(kernel, out_shape, scratch=(), near=(), flops=0, nbytes=0, trans=0, **kw):
    run = pl.pallas_call(
        kernel,
        out_shape=out_shape,
        scratch_shapes=list(scratch),
        compiler_params=pltpu.CompilerParams(vmem_limit_bytes=40 * MIB),
        cost_estimate=pl.CostEstimate(flops=flops, bytes_accessed=nbytes, transcendentals=trans),
        **kw,
    )

    def far(*args):
        return run(*[x if n in near else pltpu.with_memory_space_constraint(x, pltpu.HBM) for n, x in enumerate(args)])

    return far


VM = pl.BlockSpec(memory_space=pltpu.VMEM)
SM = pl.BlockSpec(memory_space=pltpu.SMEM)
ANY = pl.BlockSpec(memory_space=pl.ANY)


def pack_kernel(after_ref, single_ref, noisy_ref, out_ref, own_ref, scr):
    scr[...] = jnp.zeros_like(scr)
    for c in range(3):
        scr[4 * c : 4 * c + 4, 0:64] = noisy_ref[c]
    x = scr[...]
    high = x.astype(BF16).astype(F32)
    rest = x - high
    mid = rest.astype(BF16).astype(F32)
    parts = [part.astype(BF16) for part in (high, mid, rest - mid)]
    out_ref[0:64, :] = single_ref[...]
    for k in range(3):
        out_ref[64:80, 128 * k : 128 * (k + 1)] = parts[k]
        own_ref[:, 128 * k : 128 * (k + 1)] = parts[k]


def pair_rows(idx_s, chain_s, idx_v, chain_v, x_scr, table_ref):
    row_dev = lax.axis_index("dap")
    base = 32 * (2 * lax.axis_index("sch") + lax.axis_index("core"))
    lane = lane_iota((1, 128))
    odd = (row_dev % 2) == 1

    def rows_of(ref):
        row = ref[pl.ds(row_dev // 2, 1), :]
        turned = pltpu.roll(row, 64, 1)
        return jnp.where(lane < 64, jnp.where(odd, turned, row), jnp.where(odd, row, turned))

    idx_i, chain_i = rows_of(idx_v), rows_of(chain_v)
    bin_ids = lax.broadcasted_iota(jnp.int32, (table_ref.shape[0], 128), 0)

    def block(n):
        embed, rows = [], []
        for m in (2 * n, 2 * n + 1):
            idx_k = jnp.where(lane < 64, idx_s[base + m], idx_s[base + 16 + m])
            chain_k = jnp.where(lane < 64, chain_s[base + m], chain_s[base + 16 + m])
            bins = jnp.where(chain_i == chain_k, jnp.clip(idx_i - idx_k, -32, 32) + 32, 65)
            embed.append((bin_ids == bins).astype(F32).astype(BF16))
            rows += [x_scr[m], x_scr[16 + m]]
        pin = jnp.concatenate(rows, axis=0) + dot(jnp.concatenate(embed, axis=1), table_ref[...], (0, 0))
        center = pin - jnp.mean(pin, axis=-1, keepdims=True)
        spread = jnp.mean(center * center, axis=-1, keepdims=True)
        return pin, (center * lax.rsqrt(spread + 1e-5)).astype(BF16)

    return block


def pair_kernel(idx_s, chain_s, idx_v, chain_v, pair_ref, table_ref, proj_ref, msg_ref, x_scr, msg_scr):
    x_scr[...] = jnp.swapaxes(pair_ref[...].astype(F32), 0, 1)
    proj_t = jnp.transpose(proj_ref[...].astype(F32)).astype(BF16)
    block = pair_rows(idx_s, chain_s, idx_v, chain_v, x_scr, table_ref)
    for n in range(8):
        _, norm = block(n)
        projected = dot(proj_t, norm, (1, 1))
        left = sigmoid(projected[128:256]) * projected[0:128]
        right = sigmoid(projected[384:512]) * projected[256:384]
        for half in range(2):
            cols = slice(128 * half, 128 * half + 128)
            msg_scr[2 * n + half] = left[:, cols]
            msg_scr[16 + 2 * n + half] = right[:, cols]
    msg_ref[...] = jnp.swapaxes(msg_scr[...], 0, 1).astype(BF16)


def gate_kernel(after_ref, idx_s, chain_s, idx_v, chain_v, pair_ref, table_ref, gate_w_ref, pin_ref, gate_ref, x_scr):
    x_scr[...] = jnp.swapaxes(pair_ref[...].astype(F32), 0, 1)
    block = pair_rows(idx_s, chain_s, idx_v, chain_v, x_scr, table_ref)
    for n in range(8):
        pin, norm = block(n)
        pin_ref[n] = pin
        gate_ref[n] = sigmoid(dot(norm, gate_w_ref[...], (1, 0)))


def tri_kernel(msg_ref, *refs):
    out_ref, even_l, odd_l, even_r, odd_r = refs[-5:]
    for pair in range(4):
        for which, (even, odd) in enumerate(((even_l, odd_l), (even_r, odd_r))):
            a = msg_ref[32 * pair : 32 * pair + 16, 16 * which : 16 * which + 16, :]
            b = msg_ref[32 * pair + 16 : 32 * pair + 32, 16 * which : 16 * which + 16, :]
            a = a.astype(F32).reshape(256, 128)
            b = b.astype(F32).reshape(256, 128)
            low, high = swap_halves(a, b)
            even[:, 128 * pair : 128 * pair + 128] = low.astype(BF16)
            odd[:, 128 * pair : 128 * pair + 128] = high.astype(BF16)
    for pair in range(4):
        cols = slice(128 * pair, 128 * pair + 128)
        total = dot(even_r[...], even_l[:, cols], (0, 0)) + dot(odd_r[...], odd_l[:, cols], (0, 0))
        total = total.reshape(16, 2, 16, 128)
        a = total[:, 0].reshape(256, 128)
        b = total[:, 1].reshape(256, 128)
        low, high = swap_halves(a, b)
        out_ref[32 * pair : 32 * pair + 16] = low.reshape(16, 16, 128).astype(BF16)
        out_ref[32 * pair + 16 : 32 * pair + 32] = high.reshape(16, 16, 128).astype(BF16)


def update_kernel(tri_ref, pin_ref, gate_ref, tri_out_ref, bias_w_ref, after_ref, next_ref, bias_ref,
                  t_scr, x_scr, b_scr):
    t_scr[...] = jnp.swapaxes(tri_ref[...].astype(F32), 0, 1)
    for n in range(8):
        tri = jnp.concatenate([t_scr[2 * n], t_scr[2 * n + 1]], axis=1)
        center = tri - jnp.mean(tri, axis=0, keepdims=True)
        spread = jnp.mean(center * center, axis=0, keepdims=True)
        norm = (center * lax.rsqrt(spread + 1e-5)).astype(BF16)
        update = dot(norm, tri_out_ref[...], (0, 0))
        new = (pin_ref[n] + gate_ref[n] * update).astype(BF16).astype(F32)
        for half in range(2):
            x_scr[2 * n + half] = new[128 * half : 128 * half + 64]
            x_scr[16 + 2 * n + half] = new[128 * half + 64 : 128 * half + 128]
        center = new - jnp.mean(new, axis=-1, keepdims=True)
        spread = jnp.mean(center * center, axis=-1, keepdims=True)
        norm = (center * lax.rsqrt(spread + 1e-5)).astype(BF16)
        bias = dot(bias_w_ref[...], norm, (1, 1)) * LOG2E
        for half in range(2):
            b_scr[:, 2 * n + half, :] = bias[:, 128 * half : 128 * half + 128]
    next_ref[...] = jnp.swapaxes(x_scr[...], 0, 1).astype(BF16)
    for pair in range(8):
        low, high = swap_halves(b_scr[2 * pair], b_scr[2 * pair + 1])
        low, high = low.astype(BF16), high.astype(BF16)
        for n in range(bias_ref.shape[0]):
            bias_ref[n, pair, 0:16, :] = low
            bias_ref[n, pair, 16:32, :] = high


def weights_kernel(after_ref, attn_w_ref, wk_ref, wv_ref, w_scr, sems):
    width = attn_w_ref.shape[0]
    copies = []
    for n in range(2):
        cols = slice(width * (n + 1), width * (n + 2))
        copies.append(pltpu.make_async_copy(attn_w_ref.at[:, cols], w_scr.at[n], sems.at[n]))
        copies[n].start()
    copies[0].wait()
    for pair in range(8):
        cols = slice(128 * pair, 128 * pair + 96)
        wk_ref[:, cols] = w_scr[0, :, 96 * pair : 96 * pair + 96]
        wk_ref[:, 128 * pair + 96 : 128 * pair + 128] = jnp.zeros((width, 32), BF16)
    copies[1].wait()
    wv_ref[...] = jnp.transpose(w_scr[1].astype(F32)).astype(BF16)


def keys_values(act, norm_scr, wk_ref, wv_ref, k_ref, v_ref):
    spread = jnp.mean(act * act, axis=-1, keepdims=True)
    norm = (act * lax.rsqrt(spread + 1e-5)).astype(BF16)
    for d in range(8):
        for core in range(2):
            norm_scr[256 * core + 32 * d : 256 * core + 32 * d + 32, :] = norm[64 * d + 32 * core : 64 * d + 32 * core + 32]
    norm = norm_scr[...]
    for pair in range(4):
        keys = dot(norm, wk_ref[:, 256 * pair : 256 * pair + 256], (1, 0)).astype(BF16)
        k_ref[0, 2 * pair] = keys[:, 0:128]
        k_ref[0, 2 * pair + 1] = keys[:, 128:256]
    v_ref[0] = dot(wv_ref[...], norm, (1, 1)).astype(BF16)


def sample_act(smp, cond_ref, coord_ref, pos_ref):
    row = lax.broadcasted_iota(jnp.int32, pos_ref.shape, 0)
    chosen = jnp.where((row & 3) == smp, pos_ref[...], 0.0).astype(BF16)
    coords = jnp.concatenate([coord_ref[z] for z in range(4)], axis=1)
    return cond_ref[...] + dot(coords, chosen, (0, 0))


def own_rows(norm_scr):
    start = pl.multiple_of(32 * lax.axis_index("dap"), 32)
    return jnp.concatenate([norm_scr[pl.ds(start, 32), :], norm_scr[pl.ds(256 + start, 32), :]], axis=0)


def first_kernel(after_ref, types_ref, own_ref, swap_ref, type_table_ref, single_w_ref, pos_w_ref, wk_ref, wv_ref,
                 cond_ref, coord_ref, pos_ref, k_ref, v_ref, own_norm_ref, type_scr, norm_scr):
    step = pl.program_id(0)

    @pl.when(step == 0)
    def _():
        shared(types_ref, own_ref, swap_ref, type_table_ref, single_w_ref, pos_w_ref, cond_ref, coord_ref, pos_ref, type_scr)

    keys_values(sample_act(step, cond_ref, coord_ref, pos_ref), norm_scr, wk_ref, wv_ref, k_ref, v_ref)
    own_norm_ref[...] = own_rows(norm_scr)


def shared(types_ref, own_ref, swap_ref, type_table_ref, single_w_ref, pos_w_ref, cond_ref, coord_ref, pos_ref, type_scr):
    width = pos_w_ref.shape[1]
    hot = (lax.broadcasted_iota(jnp.int32, (32, 512), 0) == types_ref[...]).astype(F32).astype(BF16)
    type_scr[...] = dot(hot, type_table_ref[...], (0, 0))
    own_z, own_y = lax.axis_index("dap") // 2, lax.axis_index("dap") % 2
    own_core = lax.axis_index("core")
    low_half = lane_iota((16, 128)) < 64
    for turn in range(4):
        z = own_z ^ turn
        for swap, ref in enumerate((own_ref, swap_ref)):
            rows = pl.ds(pl.multiple_of(128 * z + 64 * (own_y ^ own_core ^ swap), 64), 64)
            feat = ref[turn, 0:64, :].astype(F32) + type_scr[rows, :]
            center = feat - jnp.mean(feat, axis=-1, keepdims=True)
            spread = jnp.mean(center * center, axis=-1, keepdims=True)
            norm = (center * lax.rsqrt(spread + 1e-5)).astype(BF16)
            cond = dot(norm, single_w_ref[...], (1, 0))
            cond_ref[rows, :] = cond - jnp.mean(cond, axis=-1, keepdims=True)
        own_first = (own_y ^ own_core) == 0
        for part in range(3):
            cols = slice(128 * part, 128 * part + 128)
            mine = own_ref[turn, 64:80, cols].astype(F32)
            mates = swap_ref[turn, 80:96, cols].astype(F32)
            first = jnp.where(own_first, mine, mates)
            second = jnp.where(own_first, mates, mine)
            both = jnp.where(low_half, first, pltpu.roll(second, 64, 1)).astype(BF16)
            for term, own in enumerate((0, 0, 1, 1, 0, 2)):
                if own == part:
                    coord_ref[z, 16 * term : 16 * term + 16, :] = both
    pos = pos_w_ref[...]
    pos = pos - jnp.mean(pos, axis=-1, keepdims=True)
    high = pos.astype(BF16).astype(F32)
    mid = (pos - high).astype(BF16).astype(F32)
    low = (pos - high - mid).astype(BF16).astype(F32)
    pos_ref[...] = jnp.zeros_like(pos_ref)
    for term, own in enumerate((0, 1, 0, 1, 2, 0)):
        for c in range(3):
            row = 16 * term + 4 * c
            pos_ref[row : row + 4, :] = jnp.broadcast_to((high, mid, low)[own][c : c + 1], (4, width))


def second_kernel(after_ref, k_before, v_before, cond_ref, coord_ref, pos_ref, wk_ref, wv_ref, own_norm_ref, attn_w_hbm,
                  k_ref, v_ref, q_ref, g_ref, norm_scr, own_scr, w_scr, sems):
    step = pl.program_id(0)
    width = wv_ref.shape[0]
    loads = [pltpu.make_async_copy(attn_w_hbm.at[:, 3 * width * n : 3 * width * n + width], w_scr.at[n], sems.at[n])
             for n in range(2)]

    @pl.when(step == 0)
    def _():
        for load in loads:
            load.start()
        own_scr[0:128, :] = own_norm_ref[...]

    keys_values(sample_act(2 + step, cond_ref, coord_ref, pos_ref), norm_scr, wk_ref, wv_ref, k_ref, v_ref)
    own_scr[pl.ds(pl.multiple_of(128 + 64 * step, 64), 64), :] = own_rows(norm_scr)

    @pl.when(step == 1)
    def _():
        own = own_scr[...]
        for load in loads:
            load.wait()
        g_ref[...] = sigmoid(dot(w_scr[1], own, (0, 1)))
        queries = dot(w_scr[0], own, (0, 1)) * (48.0 ** (-0.5) * LOG2E)
        top_rows = lax.broadcasted_iota(jnp.int32, (96, 128), 0) < 48
        low = lane_iota((96, 128)) < 64
        for pair in range(8):
            for two in range(2):
                block = queries[96 * pair : 96 * pair + 96, 128 * two : 128 * two + 128]
                turned = pltpu.roll(block, 64, 1)
                for odd in range(2):
                    first, second = (turned, block) if odd else (block, turned)
                    diagonal = jnp.where(top_rows, jnp.where(low, first, 0.0), jnp.where(low, 0.0, second))
                    q_ref[2 * two + odd, pair, 0:96, :] = diagonal.astype(BF16)
                    q_ref[2 * two + odd, pair, 96:128, :] = jnp.zeros((32, 128), BF16)


def attn_kernel(own_bias_ref, swap_bias_ref, k_ref, v_ref, q_ref, noisy_ref, coord_ref, g_hbm, act0_hbm, attn_out_hbm,
                ff_in_hbm, ff_out_hbm, out_ref, att_scr, g_ref, act0_ref, attn_out_ref, ff_in_ref, ff_out_ref, sems):
    step = pl.program_id(0)
    pairs = ((g_hbm, g_ref), (act0_hbm, act0_ref), (attn_out_hbm, attn_out_ref), (ff_in_hbm, ff_in_ref), (ff_out_hbm, ff_out_ref))
    loads = [pltpu.make_async_copy(a, b, sems.at[n]) for n, (a, b) in enumerate(pairs)]

    @pl.when(step == 0)
    def _():
        for load in loads:
            load.start()

    even = (step % 2) == 0
    straight = (lax.broadcasted_iota(jnp.int32, (96, 128), 0) < 48) == even
    mine = (lane_iota((96, 128)) < 64) == even
    own_core = lax.axis_index("core")
    chunks = []
    for swap, bias_ref in enumerate((own_bias_ref, swap_bias_ref)):
        for n in range(2):
            chunks.append((bias_ref, 4 * n, pl.ds(pl.multiple_of(256 * (own_core ^ swap) + 128 * n, 128), 128)))
    for pair in range(8):
        query = q_ref[0, pair]
        rows = slice(96 * pair, 96 * pair + 96)
        scores, tops = [], []
        for bias_ref, first, keys in chunks:
            bias = bias_ref[first : first + 4, pair].astype(F32).reshape(128, 128)
            part = dot(k_ref[0, pair, keys, :], query, (1, 0)) + bias
            scores.append(part)
            tops.append(jnp.max(part, axis=0, keepdims=True))
        top = jnp.maximum(jnp.maximum(tops[0], tops[1]), jnp.maximum(tops[2], tops[3]))
        mixed, total = 0.0, 0.0
        for part, (_, _, keys) in zip(scores, chunks):
            weights = jnp.exp2(part - top)
            total += jnp.sum(weights, axis=0, keepdims=True)
            mixed += dot(v_ref[0, rows, keys], weights.astype(BF16), (1, 0))
        attended = mixed / total
        attended = jnp.where(straight, attended, pltpu.roll(attended, 64, 1))
        att_scr[step // 2, rows, :] = jnp.where(mine, attended, att_scr[step // 2, rows, :])

    @pl.when(step == pl.num_programs(0) - 1)
    def _():
        for load in loads[:3]:
            load.wait()
        gated = (g_ref[...] * jnp.concatenate([att_scr[0], att_scr[1]], axis=1)).astype(BF16)
        act = act0_ref[...] + dot(gated, attn_out_ref[...], (0, 0))
        center = act - jnp.mean(act, axis=-1, keepdims=True)
        spread = jnp.mean(center * center, axis=-1, keepdims=True)
        norm = (center * lax.rsqrt(spread + 1e-5)).astype(BF16)
        loads[3].wait()
        loads[4].wait()
        for n in range(3):
            gate = dot(norm, ff_in_ref[:, 512 * n : 512 * n + 512], (1, 0))
            up = dot(norm, ff_in_ref[:, 1536 + 512 * n : 2048 + 512 * n], (1, 0))
            inner = (gate * sigmoid(gate) * up).astype(BF16)
            act = act + dot(inner, ff_out_ref[512 * n : 512 * n + 512, :], (1, 0))
        center = act - jnp.mean(act, axis=-1, keepdims=True)
        spread = jnp.mean(center * center, axis=-1, keepdims=True)
        final = (center * lax.rsqrt(spread + 1e-5)).astype(BF16)
        shift = dot(coord_ref[...], final, (1, 1))
        for c in range(3):
            moves = [shift[c : c + 1, 64 * n : 64 * n + 64] for n in range(4)]
            out_ref[c] = noisy_ref[c] + jnp.concatenate(moves, axis=0)


def layer_norm(values):
    center = values - jnp.mean(values, axis=-1, keepdims=True)
    spread = jnp.mean(center * center, axis=-1, keepdims=True)
    return center * lax.rsqrt(spread + 1e-05)


def condition_rows(single_rows, type_rows, type_table, single_proj):
    type_ids = jnp.arange(type_table.shape[0], dtype=jnp.int32)
    type_hot = (type_rows[:, None] == type_ids[None, :]).astype(BF16)
    token_feat = single_rows.astype(F32) + jnp.dot(type_hot, type_table, preferred_element_type=F32)
    return jnp.dot(layer_norm(token_feat).astype(BF16), single_proj, preferred_element_type=F32)


def local(
    pair_rep,
    single,
    residue_type,
    chain_id,
    residue_index,
    noisy_pos,
    type_table,
    relpos_table,
    tri_proj,
    tri_gate,
    tri_out,
    bias_proj,
    single_proj,
    pos_proj,
    attn_proj,
    attn_out,
    ff_in,
    ff_out,
    coord_out,
):
    sds = jax.ShapeDtypeStruct
    hbm = lambda shape, dtype: pltpu.HBM(shape, dtype)
    dap = lax.axis_index("dap")
    noisy = noisy_pos.transpose(1, 0, 2)

    rows_in = (residue_index, chain_id, residue_index.reshape(4, 128), chain_id.reshape(4, 128), pair_rep, relpos_table)
    rows_specs = [SM, SM, VM, VM, VM, VM]
    msg = call(
        pair_kernel, sds((128, 32, 128), BF16),
        [pltpu.VMEM((32, 64, 128), F32), pltpu.VMEM((32, 128, 128), F32)],
        flops=400_000_000, nbytes=1_700_000, trans=600_000,
        in_specs=rows_specs + [VM], out_specs=VM,
    )(*rows_in, tri_proj)
    by_channel = lax.all_to_all(msg, AXES, 0, 0, tiled=True)

    pair_in, gates = call(
        gate_kernel, (hbm((8, 256, 128), F32), hbm((8, 256, 128), F32)), [pltpu.VMEM((32, 64, 128), F32)],
        flops=130_000_000, nbytes=3_000_000, trans=300_000,
        in_specs=[ANY] + rows_specs + [VM], out_specs=(VM, VM),
    )(msg, *rows_in, tri_gate)
    packed, own_coords = call(
        pack_kernel, (sds((80, 384), BF16), sds((16, 384), BF16)), [pltpu.VMEM((16, 128), F32)], nbytes=200_000,
        in_specs=[ANY, VM, VM], out_specs=(VM, VM),
    )(msg, single, noisy)
    other_coords = lax.ppermute(own_coords, "core", [(0, 1), (1, 0)])
    block = jnp.concatenate([packed, other_coords], axis=0)
    pieces = [
        lax.ppermute(block, ("dap", "core"), [(n, n ^ (4 * turn + 2 * (n & 1))) for n in range(16)]) for turn in range(4)
    ]

    w_key, w_value = call(
        weights_kernel, (hbm((768, 1024), BF16), hbm((768, 768), BF16)),
        [pltpu.VMEM((2, 768, 768), BF16), pltpu.SemaphoreType.DMA((2,))], nbytes=5_000_000,
        in_specs=[ANY, ANY], out_specs=(VM, VM),
    )(msg, attn_proj)

    tri = call(
        tri_kernel, sds((128, 16, 128), BF16), [pltpu.VMEM((256, 512), BF16)] * 4,
        flops=270_000_000, nbytes=1_500_000, near=(0,), in_specs=[VM, ANY, ANY], out_specs=VM,
    )(by_channel, pair_in, w_key)
    tri_back = lax.all_to_all(tri, AXES, 0, 0, tiled=True)
    pieces, _ = lax.optimization_barrier((pieces, tri))
    fetched = jnp.stack(pieces)
    swapped = lax.ppermute(fetched, "core", [(0, 1), (1, 0)])

    whole = lambda shape: pl.BlockSpec(shape, lambda i: (0,) * len(shape))
    sample = lambda shape, skip=0: pl.BlockSpec((1,) + shape, lambda i: (i + skip,) + (0,) * len(shape))
    cond, coords, pos_rows, keys, values, own_norm = call(
        first_kernel,
        (hbm((512, 768), F32), hbm((4, 96, 128), BF16), hbm((96, 768), F32), hbm((4, 8, 512, 128), BF16),
         hbm((4, 768, 512), BF16), hbm((128, 768), BF16)),
        [pltpu.VMEM((512, 384), F32), pltpu.VMEM((512, 768), BF16)],
        flops=3_300_000_000, nbytes=9_000_000,
        grid=(2,),
        in_specs=[ANY, whole((1, 512)), whole((4, 96, 384)), whole((4, 96, 384)), whole((32, 384)), whole((384, 768)),
                  whole((3, 768)), whole((768, 1024)), whole((768, 768))],
        out_specs=(whole((512, 768)), whole((4, 96, 128)), whole((96, 768)), sample((8, 512, 128)), sample((768, 512)),
                   pl.BlockSpec((64, 768), lambda i: (i, 0))),
    )(tri, residue_type.reshape(1, 512), fetched, swapped, type_table, single_proj, pos_proj, w_key, w_value)

    pair_next, bias = call(
        update_kernel,
        (sds((64, 32, 128), BF16), sds((8, 8, 32, 128), BF16)),
        [pltpu.VMEM((16, 128, 128), F32), pltpu.VMEM((32, 64, 128), F32), pltpu.VMEM((16, 16, 128), F32)],
        flops=80_000_000, nbytes=4_000_000, near=(0,), in_specs=[VM] * 5 + [ANY], out_specs=(VM, VM),
    )(tri_back, pair_in, gates, tri_out, bias_proj.T, cond)
    bias_own = lax.all_to_all(bias, "sch", 0, 0, tiled=True)
    keys, values, queries, gates_own = call(
        second_kernel,
        (hbm((4, 8, 512, 128), BF16), hbm((4, 768, 512), BF16), hbm((4, 8, 128, 128), BF16), hbm((768, 256), F32)),
        [pltpu.VMEM((512, 768), BF16), pltpu.VMEM((256, 768), BF16), pltpu.VMEM((2, 768, 768), BF16),
         pltpu.SemaphoreType.DMA((2,))],
        flops=3_500_000_000, nbytes=12_000_000, trans=200_000,
        grid=(2,),
        in_specs=[ANY, ANY, ANY, whole((512, 768)), whole((4, 96, 128)), whole((96, 768)), whole((768, 1024)), whole((768, 768)),
                  whole((128, 768)), ANY],
        out_specs=(sample((8, 512, 128), 2), sample((768, 512), 2), whole((4, 8, 128, 128)), whole((768, 256))),
        input_output_aliases={1: 0, 2: 1},
    )(bias, keys, values, cond, coords, pos_rows, w_key, w_value, own_norm, attn_proj)
    bias_own, queries = lax.optimization_barrier((bias_own, queries))
    bias_swap = lax.ppermute(bias_own, "core", [(0, 1), (1, 0)])

    type_rows = lax.dynamic_slice_in_dim(residue_type, dap * 64, 64)
    condition = condition_rows(single, type_rows, type_table, single_proj)
    act0 = condition[None] + jnp.einsum("scn,ct->snt", noisy_pos, pos_proj, precision=lax.Precision.HIGHEST)
    positions = call(
        attn_kernel, sds((3, 4, 64), F32),
        [pltpu.VMEM((2, 768, 128), F32), pltpu.VMEM((768, 256), F32), pltpu.VMEM((256, 768), F32),
         pltpu.VMEM((768, 768), BF16), pltpu.VMEM((768, 3072), BF16), pltpu.VMEM((1536, 768), BF16),
         pltpu.SemaphoreType.DMA((5,))],
        near=(0, 1), flops=3_500_000_000, nbytes=18_000_000, trans=2_500_000,
        grid=(4,),
        in_specs=[whole((8, 8, 32, 128)), whole((8, 8, 32, 128)), sample((8, 512, 128)), sample((768, 512)),
                  sample((8, 128, 128)), whole((3, 4, 64)), whole((3, 768)), ANY, ANY, ANY, ANY, ANY],
        out_specs=whole((3, 4, 64)),
    )(bias_own, bias_swap, keys, values, queries, noisy, coord_out, gates_own, act0.reshape(256, 768), attn_out, ff_in, ff_out)
    return (pair_next, positions.transpose(1, 0, 2))


def solution(mesh):
    fine = Mesh(mesh.devices.reshape(8, 8, 2), AXES)
    rep = P()
    samp = ("sch", "core")
    in_specs = (P("dap", samp, None), P("dap", None), rep, rep, rep, P(samp, None, "dap")) + (rep,) * 13
    out_specs = (P("dap", samp, None), P(samp, None, "dap"))
    return jax.shard_map(local, mesh=fine, in_specs=in_specs, out_specs=out_specs, check_vma=False)
```

time: 151 us -> 96.2 us (0.64)
  waiting for transfers between devices: 34 us -> 6.13 us
  local copies, waits for them, and re-layouts: 26.2 us -> 1.52 us
  blocking collectives: 19 us -> 0 us
  Pallas kernels: 38.4 us -> 51 us
  starting transfers between devices: 26.9 us -> 33.5 us
    unnamed x78 -> x15, local copies, waits for them, and re-layouts: 26.1 us -> 0.75 us
    all_to_all x1 -> x0, blocking collectives: 19 us -> none  [local(): inputs_all = lax.all_to_all(packed, ('dap', 'core'), 0, 0, tiled=True)]
    all_to_all x2 -> x1, waiting for transfers between devices: 18.7 us -> 0.23 us  [local(): bias_own = lax.all_to_all(bias, 'sch', 0, 0, tiled=True)]
    all_to_all x1, waiting for transfers between devices: 15.3 us -> 1.5 us  [local(): by_channel = lax.all_to_all(msg, AXES, 0, 0, tiled=True)]
    pallas_call x8 -> x9, Pallas kernels: 38.4 us -> 51 us  [far(): run(*[x if n in near else pltpu.with_memory_space_constraint(x, pltpu.HBM...]
    ppermute x0 -> x7, starting transfers between devices: none -> 12.4 us  [the longest x4 7.92 us: local(): lax.ppermute(block, ('dap', 'core'), [(n, n ^ 4 * turn + 2 * (n & 1)) for...]
    all_to_all x2 -> x1, starting transfers between devices: 15 us -> 3.49 us  [local(): bias_own = lax.all_to_all(bias, 'sch', 0, 0, tiled=True)]
    all_to_all x1, starting transfers between devices: 7.28 us -> 11.5 us  [local(): by_channel = lax.all_to_all(msg, AXES, 0, 0, tiled=True)]
  transfers between devices with their start and end apart: 4 -> 10, of which waited for: 3 -> 4; matrix products, arithmetic and copies ran while one was open for 3% -> 3% of each run, Pallas kernels for 9% -> 30%
where the time goes in v2:
time: 96.2 us; the launch traced here: 95.7 us
  Pallas kernels  51 us (53%)
  starting transfers between devices  33.5 us (35%)
  waiting for transfers between devices  6.13 us (6%)
  matrix products  2.34 us (2%)
  local copies, waits for them, and re-layouts  1.52 us (2%)
  between operations  0.98 us (1%)
    pallas_call x9, Pallas kernels, far(): run(*[x if n in near else pltpu.with_memory_space_constraint(x, pltpu.HBM...  51 us
    all_to_all x1, starting transfers between devices, local(): by_channel = lax.all_to_all(msg, AXES, 0, 0, tiled=True)  11.5 us
    ppermute x4, starting transfers between devices, local(): lax.ppermute(block, ('dap', 'core'), [(n, n ^ 4 * turn + 2 * (n & 1)) for...  7.92 us
    all_to_all x1, starting transfers between devices, local(): tri_back = lax.all_to_all(tri, AXES, 0, 0, tiled=True)  6.09 us
    all_to_all x1, waiting for transfers between devices, local(): tri_back = lax.all_to_all(tri, AXES, 0, 0, tiled=True)  3.56 us
    all_to_all x1, starting transfers between devices, local(): bias_own = lax.all_to_all(bias, 'sch', 0, 0, tiled=True)  3.49 us
  transfers between devices with their start and end apart: 10, of which 4 were waited for; matrix products, arithmetic and copies ran while one was open for 3% of the time, Pallas kernels for 30%

profile of v2, /device:TPU:1, one launch (start us, length us, event | category | flops | bytes accessed | tf_op | source)
XLA Modules:
  0.0 95.7 jit_solution(7180848640309526641)
XLA Ops:
  0.6 4.9 %shard_map.194.after_ref = bf16[128,32,128]{2,1,0:T(8,128)(2,1)} custom-call(s32[512]{0:T(512)} %idx_s.3, s32[512]{0:T(512)} %chain_s.3, s32[4,128]{1,0:T(4,128)} %bitcast.23, s32[4,128]{1,0:T(4,128)} %bitcast.25, bf16[64,32,128]{2,1,0:T(8,128)(2,1)} %pair_ref.3, bf16[66,128]{1,0:T(8,128)(2,1)} %table_ref.3, bf16[128,512]{1,0:T(8,128)(2,1)} %proj_ref.1), custom_call_target="tpu_custom_call" | custom-call | flops 400000000 | bytes 1700000 | tf_op jit(solution)/shard_map/pallas_call | solution.py:43
  5.5 11.5 %all-to-all-start = ((bf16[128,32,128]{2,1,0:T(8,128)(2,1)}), bf16[128,32,128]{2,1,0:T(8,128)(2,1)S(1)}, u32[]{:S(2)}, u32[]{:S(2)}) async-start(bf16[128,32,128]{2,1,0:T(8,128)(2,1)} %shard_map.194.after_ref), calls=%async_computation | async-start | bytes 2097152 | tf_op jit(solution)/shard_map/all_to_all | solution.py:413
  17.1 0.8 shard_map.198
  17.9 1.1 %collective-permute-start = (bf16[16,384]{1,0:T(8,128)(2,1)S(1)}, bf16[16,384]{1,0:T(8,128)(2,1)S(1)}, u32[]{:S(2)}, u32[]{:S(2)}) collective-permute-start(bf16[16,384]{1,0:T(8,128)(2,1)S(1)} %get-tuple-element.30), channel_id=1, source_target_pairs={{0,1},{1,0},{2,3},{3,2},{4,5},{5,4},{6,7},{7,6},{8,9},{9,8},{10,11... | collective-permute-start | bytes 36872 | tf_op jit(solution)/shard_map/ppermute | solution.py:424
  19.0 0.8 collective-permute-done
  19.9 2.6 %collective-permute-start.1 = (bf16[96,384]{1,0:T(8,128)(2,1)S(1)}, bf16[96,384]{1,0:T(8,128)(2,1)S(1)}, u32[]{:S(2)}, u32[]{:S(2)}) collective-permute-start(bf16[96,384]{1,0:T(8,128)(2,1)S(1)} %constant_dynamic-update-slice_fusion), channel_id=1, source_target_pairs={{0,0},{1,17},{16,16},{17,1},{32,32},{33,49},{48,48},{49,33},{64,64... | collective-permute-start | bytes 221192 | tf_op jit(solution)/shard_map/ppermute | solution.py:427
  22.4 1.4 %collective-permute-start.2 = (bf16[96,384]{1,0:T(8,128)(2,1)S(1)}, bf16[96,384]{1,0:T(8,128)(2,1)S(1)}, u32[]{:S(2)}, u32[]{:S(2)}) collective-permute-start(bf16[96,384]{1,0:T(8,128)(2,1)S(1)} %constant_dynamic-update-slice_fusion), channel_id=1, source_target_pairs={{0,32},{1,49},{16,48},{17,33},{32,0},{33,17},{48,16},{49,1},{64,96... | collective-permute-start | bytes 221192 | tf_op jit(solution)/shard_map/ppermute | solution.py:427
  23.8 3.9 %collective-permute-start.3 = (bf16[96,384]{1,0:T(8,128)(2,1)S(1)}, bf16[96,384]{1,0:T(8,128)(2,1)S(1)}, u32[]{:S(2)}, u32[]{:S(2)}) collective-permute-start(bf16[96,384]{1,0:T(8,128)(2,1)S(1)} %constant_dynamic-update-slice_fusion), channel_id=1, source_target_pairs={{0,64},{1,81},{16,80},{17,65},{32,96},{33,113},{48,112},{49,97},{6... | collective-permute-start | bytes 221192 | tf_op jit(solution)/shard_map/ppermute | solution.py:427
  27.7 0.1 collective-permute-start.4
  27.8 3.8 %shard_map.196 = (bf16[768,1024]{1,0:T(8,128)(2,1)}, bf16[768,768]{1,0:T(8,128)(2,1)}) custom-call(bf16[128,32,128]{2,1,0:T(8,128)(2,1)} %shard_map.194.after_ref, bf16[768,3072]{1,0:T(8,128)(2,1)} %attn_w_hbm.1), custom_call_target="tpu_custom_call" | custom-call | bytes 5000000 | tf_op jit(solution)/shard_map/pallas_call | solution.py:43
  31.6 3.4 %shard_map.195 = (f32[8,256,128]{2,1,0:T(8,128)}, f32[8,256,128]{2,1,0:T(8,128)}) custom-call(bf16[128,32,128]{2,1,0:T(8,128)(2,1)} %shard_map.194.after_ref, s32[512]{0:T(512)} %idx_s.3, s32[512]{0:T(512)} %chain_s.3, s32[4,128]{1,0:T(4,128)} %bitcast.24, s32[4,128]{1,0:T(4,128)} %bitcast.26, bf16[64,32,128]{2,1,0:T(8,128)(2,1)} %pair_ref.3, ...), custom_call_target="tpu_custom_call" | custom-call | flops 130000000 | bytes 3000000 | tf_op jit(solution)/shard_map/pallas_call | solution.py:43
  35.0 0.0 copy-start.2
  35.0 1.5 %all-to-all-done.msg_ref = bf16[128,32,128]{2,1,0:T(8,128)(2,1)S(1)} async-done(((bf16[128,32,128]{2,1,0:T(8,128)(2,1)}), bf16[128,32,128]{2,1,0:T(8,128)(2,1)S(1)}, u32[]{:S(2)}, u32[]{:S(2)}) %all-to-all-start) | async-done | bytes 1048608 | tf_op jit(solution)/shard_map/all_to_all | solution.py:413
  36.5 2.2 %shard_map.197.after_ref = bf16[128,16,128]{2,1,0:T(8,128)(2,1)} custom-call(bf16[128,32,128]{2,1,0:T(8,128)(2,1)S(1)} %all-to-all-done.msg_ref, f32[8,256,128]{2,1,0:T(8,128)} %get-tuple-element.26.refs_0_.pin_ref, bf16[768,1024]{1,0:T(8,128)(2,1)} %get-tuple-element.27.refs_1_.wk_ref), custom_call_target="tpu_custom_call" | custom-call | flops 270000000 | bytes 1500000 | tf_op jit(solution)/shard_map/pallas_call | solution.py:43
  38.6 0.0 collective-permute-done.1
  38.6 0.0 collective-permute-done.2
  38.6 0.0 collective-permute-done.3
  38.6 0.0 collective-permute-done.4
  38.6 0.1 pad_maximum_fusion.own_ref
  38.7 0.0 copy-start.1
  38.7 1.7 %collective-permute-start.5 = (bf16[4,96,384]{2,1,0:T(8,128)(2,1)S(1)}, bf16[4,96,384]{2,1,0:T(8,128)(2,1)S(1)}, u32[]{:S(2)}, u32[]{:S(2)}) collective-permute-start(bf16[4,96,384]{2,1,0:T(8,128)(2,1)S(1)} %pad_maximum_fusion.own_ref), channel_id=1, source_target_pairs={{0,1},{1,0},{2,3},{3,2},{4,5},{5,4},{6,7},{7,6},{8,9},{9,8},{10,11... | collective-permute-start | bytes 884744 | tf_op jit(solution)/shard_map/ppermute | solution.py:443
  40.4 0.8 dynamic_slice.3
  41.1 6.1 %all-to-all-start.1 = ((bf16[128,16,128]{2,1,0:T(8,128)(2,1)}), bf16[128,16,128]{2,1,0:T(8,128)(2,1)S(1)}, u32[]{:S(2)}, u32[]{:S(2)}) async-start(bf16[128,16,128]{2,1,0:T(8,128)(2,1)} %shard_map.197.after_ref), calls=%async_computation.1 | async-start | bytes 1048576 | tf_op jit(solution)/shard_map/all_to_all | solution.py:440
  47.2 0.0 copy-done.2
  47.3 0.0 copy-done.4
  47.3 0.3 fusion.6
  47.6 0.0 collective-permute-done.5.swap_ref
  47.6 0.0 copy-start.6
  47.6 0.0 copy-done.1
  47.6 0.7 copy-done.6
  48.3 8.9 %shard_map.199 = (f32[512,768]{1,0:T(8,128)}, bf16[4,96,128]{2,1,0:T(8,128)(2,1)}, f32[96,768]{1,0:T(8,128)}, bf16[4,8,512,128]{3,2,1,0:T(8,128)(2,1)}, bf16[4,7...) custom-call(bf16[128,16,128]{2,1,0:T(8,128)(2,1)} %shard_map.197.after_ref, s32[1,512]{1,0:T(1,128)} %bitcast.29, ...), custom_call_target="tpu_custom_call" | custom-call | flops 3300000000 | bytes 9000000 | tf_op jit(solution)/shard_map/pallas_call | solution.py:43
  57.2 3.6 %all-to-all-done.1.tri_ref = bf16[128,16,128]{2,1,0:T(8,128)(2,1)S(1)} async-done(((bf16[128,16,128]{2,1,0:T(8,128)(2,1)}), bf16[128,16,128]{2,1,0:T(8,128)(2,1)S(1)}, u32[]{:S(2)}, u32[]{:S(2)}) %all-to-all-start.1) | async-done | bytes 524320 | tf_op jit(solution)/shard_map/all_to_all | solution.py:440
  60.8 4.0 %shard_map.200 = (bf16[64,32,128]{2,1,0:T(8,128)(2,1)}, bf16[8,8,32,128]{3,2,1,0:T(8,128)(2,1)}) custom-call(bf16[128,16,128]{2,1,0:T(8,128)(2,1)S(1)} %all-to-all-done.1.tri_ref, f32[8,256,128]{2,1,0:T(8,128)} %get-tuple-element.26.refs_0_.pin_ref, f32[8,256,128]{2,1,0:T(8,128)} %get-tuple-element.28.gate_ref, bf16[128,128]{1,0:T(8,128)(2,1)} %tri_out_ref.1, ...), custom_call_target="tpu_custom_call" | custom-call | flops 80000000 | bytes 4000000 | tf_op jit(solution)/shard_map/pallas_call | solution.py:43
  64.8 3.5 %all-to-all-start.2 = ((bf16[8,8,32,128]{3,2,1,0:T(8,128)(2,1)}), bf16[8,8,32,128]{3,2,1,0:T(8,128)(2,1)S(1)}, u32[]{:S(2)}, u32[]{:S(2)}) async-start(bf16[8,8,32,128]{3,2,1,0:T(8,128)(2,1)} %get-tuple-element.38.after_ref), calls=%async_computation.2 | async-start | bytes 1048576 | tf_op jit(solution)/shard_map/all_to_all | solution.py:466
  68.3 0.2 multiply_reduce_fusion
  68.5 0.0 copy-start
  68.5 0.0 copy-start.3
  68.5 0.0 copy-start.5
  68.5 9.6 %shard_map.201 = (bf16[4,8,512,128]{3,2,1,0:T(8,128)(2,1)}, bf16[4,768,512]{2,1,0:T(8,128)(2,1)}, bf16[4,8,128,128]{3,2,1,0:T(8,128)(2,1)}, f32[768,256]{1,0:T(8,128)}) custom-call(bf16[8,8,32,128]{3,2,1,0:T(8,128)(2,1)} %get-tuple-element.38.after_ref, ...), custom_call_target="tpu_custom_call", output_to_operand_aliasing={{0}: (1, {}), {1}: (2, {})} | custom-call | flops 3500000000 | bytes 12000000 | tf_op jit(solution)/shard_map/pallas_call | solution.py:43
  78.2 0.2 all-to-all-done.2.own_bias_ref
  78.4 1.7 %collective-permute-start.6 = (bf16[8,8,32,128]{3,2,1,0:T(8,128)(2,1)S(1)}, bf16[8,8,32,128]{3,2,1,0:T(8,128)(2,1)S(1)}, u32[]{:S(2)}, u32[]{:S(2)}) collective-permute-start(bf16[8,8,32,128]{3,2,1,0:T(8,128)(2,1)S(1)} %all-to-all-done.2.own_bias_ref), channel_id=1, source_target_pairs={{0,1},{1,0},{2,3},{3,2},{4,5},{5,4},{6,7},{7,6},{8,9},{9,8},{10,11... | collective-permute-start | bytes 1572872 | tf_op jit(solution)/shard_map/ppermute | solution.py:480
  80.1 0.0 copy-done
  80.1 0.3 fusion
  80.3 0.0 copy-done.3
  80.4 0.0 copy-done.5
  80.4 1.8 %convolution_add_fusion = f32[4,64,768]{2,1,0:T(8,128)} fusion(f32[64,768]{1,0:T(8,128)S(1)} %fusion, f32[3,768]{1,0:T(4,128)S(1)} %copy-done.5, f32[4,3,64]{2,0,1:T(4,128)S(1)} %copy-done.3), kind=kOutput, calls=%fused_computation | convolution fusion | flops 7274496 | bytes 995328 | tf_op jit(solution)/shard_map/scn,ct->snt/dot_general | solution.py:484
  82.1 0.0 collective-permute-done.6.swap_bias_ref
  82.1 13.4 %shard_map.202 = f32[3,4,64]{2,1,0:T(4,128)} custom-call(bf16[8,8,32,128]{3,2,1,0:T(8,128)(2,1)S(1)} %all-to-all-done.2.own_bias_ref, bf16[8,8,32,128]{3,2,1,0:T(8,128)(2,1)S(1)} %collective-permute-done.6.swap_bias_ref, bf16[4,8,512,128]{3,2,1,0:T(8,128)(2,1)} %get-tuple-element.46.k_ref, bf16[4,768,512]{2,1,0:T(8,128)(2,1)} %get-tuple-element.47.v_ref, ...), custom_call_target="tpu_custom_call" | custom-call | flops 3500000000 | bytes 18000000 | tf_op jit(solution)/shard_map/pallas_call | solution.py:43
  (5 shorter events, 0.0 us)
Async XLA Ops:
  5.5 30.9 %all-to-all-start = ((bf16[128,32,128]{2,1,0:T(8,128)(2,1)}), bf16[128,32,128]{2,1,0:T(8,128)(2,1)S(1)}, u32[]{:S(2)}, u32[]{:S(2)}) async-start(bf16[128,32,128]{2,1,0:T(8,128)(2,1)} %shard_map.194.after_ref), calls=%async_computation | async-start | bytes 2097152 | tf_op jit(solution)/shard_map/all_to_all | solution.py:413
  17.9 2.0 %collective-permute-start = (bf16[16,384]{1,0:T(8,128)(2,1)S(1)}, bf16[16,384]{1,0:T(8,128)(2,1)S(1)}, u32[]{:S(2)}, u32[]{:S(2)}) collective-permute-start(bf16[16,384]{1,0:T(8,128)(2,1)S(1)} %get-tuple-element.30), channel_id=1, source_target_pairs={{0,1},{1,0},{2,3},{3,2},{4,5},{5,4},{6,7},{7,6},{8,9},{9,8},{10,11... | collective-permute-start | bytes 36872 | tf_op jit(solution)/shard_map/ppermute | solution.py:424
  19.9 18.8 %collective-permute-start.1 = (bf16[96,384]{1,0:T(8,128)(2,1)S(1)}, bf16[96,384]{1,0:T(8,128)(2,1)S(1)}, u32[]{:S(2)}, u32[]{:S(2)}) collective-permute-start(bf16[96,384]{1,0:T(8,128)(2,1)S(1)} %constant_dynamic-update-slice_fusion), channel_id=1, source_target_pairs={{0,0},{1,17},{16,16},{17,1},{32,32},{33,49},{48,48},{49,33},{64,64... | collective-permute-start | bytes 221192 | tf_op jit(solution)/shard_map/ppermute | solution.py:427
  22.4 16.2 %collective-permute-start.2 = (bf16[96,384]{1,0:T(8,128)(2,1)S(1)}, bf16[96,384]{1,0:T(8,128)(2,1)S(1)}, u32[]{:S(2)}, u32[]{:S(2)}) collective-permute-start(bf16[96,384]{1,0:T(8,128)(2,1)S(1)} %constant_dynamic-update-slice_fusion), channel_id=1, source_target_pairs={{0,32},{1,49},{16,48},{17,33},{32,0},{33,17},{48,16},{49,1},{64,96... | collective-permute-start | bytes 221192 | tf_op jit(solution)/shard_map/ppermute | solution.py:427
  23.8 14.8 %collective-permute-start.3 = (bf16[96,384]{1,0:T(8,128)(2,1)S(1)}, bf16[96,384]{1,0:T(8,128)(2,1)S(1)}, u32[]{:S(2)}, u32[]{:S(2)}) collective-permute-start(bf16[96,384]{1,0:T(8,128)(2,1)S(1)} %constant_dynamic-update-slice_fusion), channel_id=1, source_target_pairs={{0,64},{1,81},{16,80},{17,65},{32,96},{33,113},{48,112},{49,97},{6... | collective-permute-start | bytes 221192 | tf_op jit(solution)/shard_map/ppermute | solution.py:427
  27.7 10.9 %collective-permute-start.4 = (bf16[96,384]{1,0:T(8,128)(2,1)S(1)}, bf16[96,384]{1,0:T(8,128)(2,1)S(1)}, u32[]{:S(2)}, u32[]{:S(2)}) collective-permute-start(bf16[96,384]{1,0:T(8,128)(2,1)S(1)} %constant_dynamic-update-slice_fusion), channel_id=1, source_target_pairs={{0,96},{1,113},{16,112},{17,97},{32,64},{33,81},{48,80},{49,65},{6... | collective-permute-start | bytes 221192 | tf_op jit(solution)/shard_map/ppermute | solution.py:427
  35.0 12.3 %copy-start.2 = (bf16[64,384]{1,0:T(8,128)(2,1)S(1)}, bf16[64,384]{1,0:T(8,128)(2,1)}, u32[]{:S(2)}) copy-start(bf16[64,384]{1,0:T(8,128)(2,1)} %single_ref.1) | copy-start | bytes 147460
  35.0 12.3 %copy-start.4 = (bf16[32,384]{1,0:T(8,128)(2,1)S(1)}, bf16[32,384]{1,0:T(8,128)(2,1)}, u32[]{:S(2)}) copy-start(bf16[32,384]{1,0:T(8,128)(2,1)} %type_table_ref.1) | copy-start | bytes 73732
  38.7 8.9 %copy-start.1 = (bf16[4,96,384]{2,1,0:T(8,128)(2,1)}, bf16[4,96,384]{2,1,0:T(8,128)(2,1)S(1)}, u32[]{:S(2)}) copy-start(bf16[4,96,384]{2,1,0:T(8,128)(2,1)S(1)} %pad_maximum_fusion.own_ref) | copy-start | bytes 884740
  38.7 8.9 %collective-permute-start.5 = (bf16[4,96,384]{2,1,0:T(8,128)(2,1)S(1)}, bf16[4,96,384]{2,1,0:T(8,128)(2,1)S(1)}, u32[]{:S(2)}, u32[]{:S(2)}) collective-permute-start(bf16[4,96,384]{2,1,0:T(8,128)(2,1)S(1)} %pad_maximum_fusion.own_ref), channel_id=1, source_target_pairs={{0,1},{1,0},{2,3},{3,2},{4,5},{5,4},{6,7},{7,6},{8,9},{9,8},{10,11... | collective-permute-start | bytes 884744 | tf_op jit(solution)/shard_map/ppermute | solution.py:443
  41.1 19.6 %all-to-all-start.1 = ((bf16[128,16,128]{2,1,0:T(8,128)(2,1)}), bf16[128,16,128]{2,1,0:T(8,128)(2,1)S(1)}, u32[]{:S(2)}, u32[]{:S(2)}) async-start(bf16[128,16,128]{2,1,0:T(8,128)(2,1)} %shard_map.197.after_ref), calls=%async_computation.1 | async-start | bytes 1048576 | tf_op jit(solution)/shard_map/all_to_all | solution.py:440
  47.6 0.7 copy-start.6
  64.8 13.6 %all-to-all-start.2 = ((bf16[8,8,32,128]{3,2,1,0:T(8,128)(2,1)}), bf16[8,8,32,128]{3,2,1,0:T(8,128)(2,1)S(1)}, u32[]{:S(2)}, u32[]{:S(2)}) async-start(bf16[8,8,32,128]{3,2,1,0:T(8,128)(2,1)} %get-tuple-element.38.after_ref), calls=%async_computation.2 | async-start | bytes 1048576 | tf_op jit(solution)/shard_map/all_to_all | solution.py:466
  68.5 11.6 %copy-start = (bf16[384,768]{1,0:T(8,128)(2,1)S(1)}, bf16[384,768]{1,0:T(8,128)(2,1)}, u32[]{:S(2)}) copy-start(bf16[384,768]{1,0:T(8,128)(2,1)} %single_w_ref.1) | copy-start | bytes 1769476
  68.5 11.9 %copy-start.3 = (f32[4,3,64]{2,0,1:T(4,128)S(1)}, f32[4,3,64]{2,0,1:T(4,128)}, u32[]{:S(2)}) copy-start(f32[4,3,64]{2,0,1:T(4,128)} %param.24) | copy-start | bytes 9220
  68.5 11.9 %copy-start.5 = (f32[3,768]{1,0:T(4,128)S(1)}, f32[3,768]{1,0:T(4,128)}, u32[]{:S(2)}) copy-start(f32[3,768]{1,0:T(4,128)} %pos_w_ref.1) | copy-start | bytes 27652
  78.4 3.8 %collective-permute-start.6 = (bf16[8,8,32,128]{3,2,1,0:T(8,128)(2,1)S(1)}, bf16[8,8,32,128]{3,2,1,0:T(8,128)(2,1)S(1)}, u32[]{:S(2)}, u32[]{:S(2)}) collective-permute-start(bf16[8,8,32,128]{3,2,1,0:T(8,128)(2,1)S(1)} %all-to-all-done.2.own_bias_ref), channel_id=1, source_target_pairs={{0,1},{1,0},{2,3},{3,2},{4,5},{5,4},{6,7},{7,6},{8,9},{9,8},{10,11... | collective-permute-start | bytes 1572872 | tf_op jit(solution)/shard_map/ppermute | solution.py:480
